TPU v7x, 128 devices: a whole 4x4x4 slice. The times are simulated.
128 devices in a mesh: fsdp: 128 (over y, x, z, core).
Axes of the slice: x: 4, y: 4, z: 4, core: 2. Of those that a mesh axis runs over, the one named last changes fastest.
Arguments:
- momentum: float32 [64, 1024, 3584], P(None, 'fsdp'), may hold values from -40 to 40
- gradient: bfloat16 [64, 1024, 3584], P(None, 'fsdp'), may hold values from -40 to 40
Outputs:
- new_momentum: float32 [64, 1024, 3584], P(None, 'fsdp')
- update: bfloat16 [64, 1024, 3584], P(None, 'fsdp')
All inputs are finite; a program needn't handle non-finite values.
Results may differ from a plain program's by a relative error of at most 0.02.
Values may be sent and summed in bfloat16 or wider, within the bound.
No kernel may reach another device: no remote copies, remote signals or barrier semaphores. Data moves between devices by JAX's collectives and lax.ppermute only.
A program may use at most 128 MiB of HBM per device.

v0:
```python
import jax
import jax.numpy as jnp
from jax import lax
from jax.sharding import PartitionSpec as P

D = 3584
FF = 1024
ITERS = 3


def partner(x, axis, apart):
    return lax.ppermute(x, axis, [(i, i ^ 1 << apart) for i in range(lax.axis_size(axis))])


def local(momentum, gradient):
    count = lax.axis_size("fsdp")
    mats, rows, width = momentum.shape
    half = width // 2
    new_momentum = 0.95 * momentum + gradient.astype(jnp.float32)
    steer = (gradient.astype(jnp.float32) + 0.95 * new_momentum).astype(jnp.bfloat16)
    pieces = steer.reshape(mats, rows, 2, half).transpose(0, 2, 1, 3).reshape(mats * 2, rows, half)
    owned = lax.all_to_all(pieces, "fsdp", split_axis=0, concat_axis=1, tiled=True)[0]
    owned_f = owned.astype(jnp.float32)
    own_sum = jnp.sum(owned_f * owned_f)
    total = own_sum + partner(own_sum, "fsdp", 0)
    inverse = 1.0 / (jnp.sqrt(total) + 1e-07)
    x = (owned_f * inverse).astype(jnp.bfloat16)
    for step in range(ITERS):
        partial_gram = lax.dot_general(
            x, x, (((1,), (1,)), ((), ())), preferred_element_type=jnp.float32
        )
        gram = (partial_gram + partner(partial_gram, "fsdp", 0)).astype(jnp.bfloat16)
        square = jnp.dot(gram, gram, preferred_element_type=jnp.float32)
        mix = (-4.775 * gram.astype(jnp.float32) + 2.0315 * square).astype(jnp.bfloat16)
        x = (
            3.4445 * x.astype(jnp.float32) + jnp.dot(mix, x, preferred_element_type=jnp.float32)
        ).astype(jnp.bfloat16)
    factor = 0.2 * max(FF, D) ** 0.5
    scaled = (x.astype(jnp.float32) * factor).astype(jnp.bfloat16)
    outgoing = scaled.reshape(count, rows, half)
    returned = lax.all_to_all(outgoing, "fsdp", split_axis=0, concat_axis=0, tiled=True)
    update = returned.reshape(mats, 2, rows, half).transpose(0, 2, 1, 3).reshape(mats, rows, width)
    return (new_momentum, update)


def solution(mesh):
    return jax.shard_map(
        local,
        mesh=mesh,
        in_specs=(P(None, "fsdp", None), P(None, "fsdp", None)),
        out_specs=(P(None, "fsdp", None), P(None, "fsdp", None)),
        check_vma=False,
    )
```

profile of v0, /device:TPU:1, one launch (start us, length us, event | category | flops | bytes accessed | tf_op | source)
XLA Modules:
  0.0 218.2 jit_solution(5663658598096298921)
XLA Ops:
  0.6 8.7 %fusion = (bf16[64,8,3584]{2,1,0:T(8,128)(2,1)S(1)}, f32[64,8,3584]{2,1,0:T(8,128)}) fusion(bf16[64,8,3584]{2,1,0:T(8,128)(2,1)} %param.3, f32[64,8,3584]{2,1,0:T(8,128)} %param.2), kind=kLoop, calls=%fused_computation.4 | loop fusion | flops 11010048 | bytes 22020096 | tf_op jit(solution)/shard_map/convert_element_type | solution.py:20
  9.6 0.3 pad_maximum_fusion
  9.9 58.4 %all_to_all.14 = bf16[128,8,1792]{2,1,0:T(8,128)(2,1)S(1)} all-to-all(bf16[128,8,1792]{2,1,0:T(8,128)(2,1)S(1)} %bitcast.22), channel_id=1, replica_groups=mesh['fsdp'=128] {'fsdp'}, dimensions={0} | all-to-all | bytes 7340032 | tf_op jit(solution)/shard_map/all_to_all | solution.py:22
  68.2 1.8 copy-done
  70.1 2.6 %fusion.1 = f32[]{:T(128)} fusion(bf16[128,8,1792]{2,1,0:T(8,128)(2,1)S(1)} %all_to_all.14), kind=kLoop, calls=%fused_computation.5 | loop fusion | flops 5505023 | bytes 3670020 | tf_op jit(solution)/shard_map/reduce_sum | solution.py:24
  72.6 1.3 collective-permute-start
  73.9 0.9 collective-permute-done
  76.2 7.2 %fusion.5 = f32[1024,1024]{1,0:T(8,128)S(1)} fusion(bf16[128,8,1792]{2,1,0:T(8,128)(2,1)} %copy-done, f32[]{:T(128)S(6)} %div.3), kind=kOutput, calls=%fused_computation.20 | convolution fusion | flops 3763601408 | bytes 7864324 | tf_op jit(solution)/shard_map/dot_general | solution.py:29
  83.4 0.5 collective-permute-start.1
  83.9 6.9 %collective-permute-done.1 = f32[1024,1024]{1,0:T(8,128)S(1)} collective-permute-done((f32[1024,1024]{1,0:T(8,128)S(1)}, f32[1024,1024]{1,0:T(8,128)S(1)}, u32[]{:S(2)}, u32[]{:S(2)}) %collective-permute-start.1) | collective-permute-done | bytes 4194336 | tf_op jit(solution)/shard_map/ppermute | solution.py:12
  90.8 2.7 %add_convert_fusion.7 = bf16[1024,1024]{1,0:T(8,128)(2,1)S(1)} fusion(f32[1024,1024]{1,0:T(8,128)S(1)} %fusion.5, f32[1024,1024]{1,0:T(8,128)S(1)} %collective-permute-done.1), kind=kOutput, calls=%fused_computation.15 | convolution fusion | flops 2156920832 | bytes 10485760 | tf_op jit(solution)/shard_map/dot_general | solution.py:33
  93.5 4.5 %add_convert_fusion.2 = bf16[1024,1792]{1,0:T(8,128)(2,1)S(1)} fusion(bf16[1024,1024]{1,0:T(8,128)(2,1)S(1)} %add_convert_fusion.7, f32[]{:T(128)S(6)} %div.3, bf16[128,8,1792]{2,1,0:T(8,128)(2,1)S(1)} %copy-done.1), kind=kOutput, calls=%fused_computation.10 | convolution fusion | flops 3776446464 | bytes 9437188 | tf_op jit(solution)/shard_map/dot_general | solution.py:36
  98.0 4.0 %fusion.13 = f32[1024,1024]{1,0:T(8,128)S(1)} fusion(bf16[1024,1792]{1,0:T(8,128)(2,1)S(1)} %add_convert_fusion.2), kind=kOutput, calls=%fused_computation.26 | convolution fusion | flops 3758096384 | bytes 7864320 | tf_op jit(solution)/shard_map/dot_general | solution.py:29
  102.0 1.9 copy-done.2
  103.9 0.3 collective-permute-start.2
  104.2 7.0 %collective-permute-done.2 = f32[1024,1024]{1,0:T(8,128)} collective-permute-done((f32[1024,1024]{1,0:T(8,128)S(1)}, f32[1024,1024]{1,0:T(8,128)}, u32[]{:S(2)}, u32[]{:S(2)}) %collective-permute-start.2) | collective-permute-done | bytes 4194336 | tf_op jit(solution)/shard_map/ppermute | solution.py:12
  111.2 18.7 %add_convert_fusion.1 = bf16[1024,1792]{1,0:T(8,128)(2,1)} fusion(bf16[1024,1792]{1,0:T(8,128)(2,1)} %copy-done.4, f32[1024,1024]{1,0:T(8,128)} %copy-done.2, f32[1024,1024]{1,0:T(8,128)} %collective-permute-done.2), kind=kOutput, calls=%fused_computation.9 | convolution fusion | flops 5922357248 | bytes 15728640 | tf_op jit(solution)/shard_map/dot_general | solution.py:36
  130.0 7.1 %fusion.14 = f32[1024,1024]{1,0:T(8,128)S(1)} fusion(bf16[1024,1792]{1,0:T(8,128)(2,1)} %add_convert_fusion.1), kind=kOutput, calls=%fused_computation.27 | convolution fusion | flops 3758096384 | bytes 7864320 | tf_op jit(solution)/shard_map/dot_general | solution.py:29
  137.1 1.9 copy-done.3
  139.1 0.3 collective-permute-start.3
  139.3 7.0 %collective-permute-done.3 = f32[1024,1024]{1,0:T(8,128)} collective-permute-done((f32[1024,1024]{1,0:T(8,128)S(1)}, f32[1024,1024]{1,0:T(8,128)}, u32[]{:S(2)}, u32[]{:S(2)}) %collective-permute-start.3) | collective-permute-done | bytes 4194336 | tf_op jit(solution)/shard_map/ppermute | solution.py:12
  146.3 18.9 %fusion.3 = bf16[128,8,1792]{2,1,0:T(8,128)(2,1)} fusion(bf16[1024,1792]{1,0:T(8,128)(2,1)} %add_convert_fusion.1, f32[1024,1024]{1,0:T(8,128)} %copy-done.3, f32[1024,1024]{1,0:T(8,128)} %collective-permute-done.3), kind=kOutput, calls=%fused_computation.17 | convolution fusion | flops 5927862272 | bytes 15728640 | tf_op jit(solution)/shard_map/dot_general | solution.py:36
  165.2 51.2 %all_to_all.15 = bf16[128,8,1792]{2,1,0:T(8,128)(2,1)S(1)} all-to-all(bf16[128,8,1792]{2,1,0:T(8,128)(2,1)} %fusion.3), channel_id=1, replica_groups=mesh['fsdp'=128] {'fsdp'}, dimensions={0} | all-to-all | bytes 7340032 | tf_op jit(solution)/shard_map/all_to_all | solution.py:41
  216.4 1.8 copy.5
  (8 shorter events, 0.3 us)
Async XLA Ops:
  68.2 1.8 copy-start
  72.6 2.2 %collective-permute-start = (f32[]{:T(128)}, f32[]{:T(128)}, u32[]{:S(2)}, u32[]{:S(2)}) collective-permute-start(f32[]{:T(128)} %fusion.1), channel_id=1, source_target_pairs={{0,1},{1,0},{2,3},{3,2},{4,5},{5,4},{6,7},{7,6},{8,9},{9,8},{10,11... | collective-permute-start | bytes 20 | tf_op jit(solution)/shard_map/ppermute | solution.py:12
  83.4 10.1 %copy-start.1 = (bf16[128,8,1792]{2,1,0:T(8,128)(2,1)S(1)}, bf16[128,8,1792]{2,1,0:T(8,128)(2,1)}, u32[]{:S(2)}) copy-start(bf16[128,8,1792]{2,1,0:T(8,128)(2,1)} %copy-done) | copy-start | bytes 11010052
  83.4 7.4 %collective-permute-start.1 = (f32[1024,1024]{1,0:T(8,128)S(1)}, f32[1024,1024]{1,0:T(8,128)S(1)}, u32[]{:S(2)}, u32[]{:S(2)}) collective-permute-start(f32[1024,1024]{1,0:T(8,128)S(1)} %fusion.5), channel_id=1, source_target_pairs={{0,1},{1,0},{2,3},{3,2},{4,5},{5,4},{6,7},{7,6},{8,9},{9,8},{10,11... | collective-permute-start | bytes 12582920 | tf_op jit(solution)/shard_map/ppermute | solution.py:12
  98.0 4.0 %copy-start.4 = (bf16[1024,1792]{1,0:T(8,128)(2,1)}, bf16[1024,1792]{1,0:T(8,128)(2,1)S(1)}, u32[]{:S(2)}) copy-start(bf16[1024,1792]{1,0:T(8,128)(2,1)S(1)} %add_convert_fusion.2) | copy-start | bytes 11010052
  102.0 1.9 copy-start.2
  103.9 7.3 %collective-permute-start.2 = (f32[1024,1024]{1,0:T(8,128)S(1)}, f32[1024,1024]{1,0:T(8,128)}, u32[]{:S(2)}, u32[]{:S(2)}) collective-permute-start(f32[1024,1024]{1,0:T(8,128)S(1)} %fusion.13), channel_id=1, source_target_pairs={{0,1},{1,0},{2,3},{3,2},{4,5},{5,4},{6,7},{7,6},{8,9},{9,8},{10,11... | collective-permute-start | bytes 12582920 | tf_op jit(solution)/shard_map/ppermute | solution.py:12
  137.1 1.9 copy-start.3
  139.1 7.3 %collective-permute-start.3 = (f32[1024,1024]{1,0:T(8,128)S(1)}, f32[1024,1024]{1,0:T(8,128)}, u32[]{:S(2)}, u32[]{:S(2)}) collective-permute-start(f32[1024,1024]{1,0:T(8,128)S(1)} %fusion.14), channel_id=1, source_target_pairs={{0,1},{1,0},{2,3},{3,2},{4,5},{5,4},{6,7},{7,6},{8,9},{9,8},{10,11... | collective-permute-start | bytes 12582920 | tf_op jit(solution)/shard_map/ppermute | solution.py:12
where the time goes:
time: 218 us
  blocking collectives  110 us (50%)
  matrix products  63.1 us (29%)
  waiting for transfers between devices  21.8 us (10%)
  other arithmetic  11.5 us (5%)
  local copies, waits for them, and re-layouts  7.78 us (4%)
  starting transfers between devices  2.38 us (1%)
    all_to_all x1, blocking collectives, local(): lax.all_to_all(pieces, 'fsdp', split_axis=0, concat_axis=1, tiled=True)[0]  58.4 us
    all_to_all x1, blocking collectives, local(): lax.all_to_all(outgoing, 'fsdp', split_axis=0, concat_axis=0, tiled=True)  51.2 us
    dot_general x3, matrix products, local(): jnp.dot(mix, x, preferred_element_type=jnp.float32)  42.1 us
    ppermute x4, waiting for transfers between devices, partner(): lax.ppermute(x, axis, [(i, i ^ 1 << apart) for i in range(lax.axis_size(a...  21.8 us
    dot_general x3, matrix products, local(): lax.dot_general(x, x, (((1,), (1,)), ((), ())), preferred_element_type=jn...  18.3 us
    convert_element_type x1, other arithmetic, local(): (gradient.astype(jnp.float32) + 0.95 * new_momentum).astype(jnp.bfloat16)  8.72 us
    unnamed x11, local copies, waits for them, and re-layouts  7.54 us
  transfers between devices with their start and end apart: 4, of which 4 were waited for; matrix products, arithmetic and copies ran while one was open for 0% of the time, Pallas kernels for 0%

commit v1 on v0

v1 whole, which is shorter than its diff:
```python
import jax
import jax.numpy as jnp
from jax import lax
from jax.experimental import pallas as pl
from jax.experimental.pallas import tpu as pltpu
from jax.sharding import PartitionSpec as P

D = 3584
FF = 1024
ITERS = 3
LINEAR, CUBIC, QUINTIC = 3.4445, -4.775, 2.0315
FACTOR = 0.2 * max(FF, D) ** 0.5
TILE = 256
SIDE = FF // TILE
PAIRS = [(i, j) for j in range(SIDE) for i in range(j + 1)]
MIB = 2**20


def cost(flops, moved):
    return pl.CostEstimate(flops=flops, bytes_accessed=moved, transcendentals=0)


def span(i, size=TILE):
    return slice(i * size, (i + 1) * size)


def partner(x, axis, apart):
    return lax.ppermute(x, axis, [(i, i ^ 1 << apart) for i in range(lax.axis_size(axis))])


STEER_PARTS = 8


def steer_kernel(momentum, gradient, steer, m_buf, g_buf, s_buf, m_sem, g_sem, s_sem):
    mats, rows, width = m_buf.shape
    half = width // 2
    group = mats // STEER_PARTS
    arriving = []
    for c in range(STEER_PARTS):
        at = pl.ds(c * group, group)
        pair = (
            pltpu.make_async_copy(momentum.at[at], m_buf.at[at], m_sem.at[c]),
            pltpu.make_async_copy(gradient.at[at], g_buf.at[at], g_sem.at[c]),
        )
        for copy in pair:
            copy.start()
        arriving.append(pair)
    leaving = []
    for c in range(STEER_PARTS):
        for copy in arriving[c]:
            copy.wait()

        @pl.loop(c * group, (c + 1) * group)
        def _(m):
            g = g_buf[m].astype(jnp.float32)
            moved = 0.95 * m_buf[m] + g
            value = (g + 0.95 * moved).astype(jnp.bfloat16)
            s_buf[m, 0] = value[:, :half]
            s_buf[m, 1] = value[:, half:]

        at = pl.ds(c * group, group)
        copy = pltpu.make_async_copy(s_buf.at[at], steer.at[at], s_sem.at[c])
        copy.start()
        leaving.append(copy)
    for copy in leaving:
        copy.wait()


def steer_pieces(momentum, gradient):
    mats, rows, width = momentum.shape
    shape = (mats, 2, rows, width // 2)
    anywhere = pl.BlockSpec(memory_space=pl.ANY)
    dma = pltpu.SemaphoreType.DMA((STEER_PARTS,))
    return pl.pallas_call(
        steer_kernel,
        out_shape=jax.ShapeDtypeStruct(shape, jnp.bfloat16),
        in_specs=[anywhere] * 2,
        out_specs=anywhere,
        scratch_shapes=[
            pltpu.VMEM(momentum.shape, jnp.float32),
            pltpu.VMEM(gradient.shape, jnp.bfloat16),
            pltpu.VMEM(shape, jnp.bfloat16),
            dma,
            dma,
            dma,
        ],
        compiler_params=pltpu.CompilerParams(vmem_limit_bytes=56 * MIB),
        cost_estimate=cost(4 * momentum.size, 8 * momentum.size),
        name="steer",
    )(momentum, gradient).reshape(mats * 2, rows, width // 2)


def gram_kernel(x, own, sent, x_buf, sem):
    arriving = []
    for i in range(SIDE):
        copy = pltpu.make_async_copy(x.at[span(i)], x_buf.at[span(i)], sem.at[i])
        copy.start()
        arriving.append(copy)
    for j in range(SIDE):
        arriving[j].wait()
        value = lax.dot_general(
            x_buf[0 : (j + 1) * TILE],
            x_buf[span(j)],
            (((1,), (1,)), ((), ())),
            preferred_element_type=jnp.float32,
        )
        at = slice(j * (j + 1) // 2 * TILE, (j + 1) * (j + 2) // 2 * TILE)
        own[at] = value
        sent[at] = value.astype(jnp.bfloat16)


def gram_half(x):
    rows, part = x.shape
    shape = (len(PAIRS) * TILE, TILE)
    return pl.pallas_call(
        gram_kernel,
        out_shape=(
            jax.ShapeDtypeStruct(shape, jnp.float32),
            jax.ShapeDtypeStruct(shape, jnp.bfloat16),
        ),
        in_specs=[pl.BlockSpec(memory_space=pl.ANY)],
        scratch_shapes=[
            pltpu.VMEM((rows, part), jnp.bfloat16),
            pltpu.SemaphoreType.DMA((SIDE,)),
        ],
        compiler_params=pltpu.CompilerParams(vmem_limit_bytes=32 * MIB),
        cost_estimate=cost(2 * len(PAIRS) * TILE * TILE * part, rows * part * 2 + len(PAIRS) * TILE * TILE * 6),
        name="gram",
    )(x)


def update_kernel(x, own, other, out, x_buf, g, h, s, w, m0, m1, x_sem):
    n, part = x_buf.shape
    loading = pltpu.make_async_copy(x, x_buf, x_sem)
    loading.start()
    here = lax.broadcasted_iota(jnp.int32, (TILE, TILE), 0) == lax.broadcasted_iota(
        jnp.int32, (TILE, TILE), 1
    )
    total = jnp.zeros((1, 1), jnp.float32)
    for k, (i, j) in enumerate(PAIRS):
        block = own[span(k)] + other[span(k)].astype(jnp.float32)
        narrow = block.astype(jnp.bfloat16)
        g[span(i), span(j)] = narrow
        if i == j:
            block = jnp.where(here, block, 0.0)
            block = jnp.sum(block, axis=0, keepdims=True)
            total = total + jnp.sum(block, axis=1, keepdims=True)
        else:
            g[span(j), span(i)] = narrow.T
    inverse = 1.0 / (jnp.sqrt(total) + 1e-07)
    factor = inverse * FACTOR
    square = inverse * inverse

    def product(left, right, store, rest):
        for j in range(SIDE):
            at = (slice(0, (j + 1) * TILE), span(j))
            value = jnp.dot(left[at[0], :], right[:, at[1]], preferred_element_type=jnp.float32)
            narrow = rest(value, at).astype(jnp.bfloat16)
            store[at] = narrow
            for i in range(j):
                store[span(j), span(i)] = narrow[span(i)].T

    def wide(ref, at):
        return ref[at].astype(jnp.float32)


    product(g, g, m0, lambda v, at: square * (CUBIC * wide(g, at) + square * (QUINTIC * v)))
    product(m0, g, w, lambda v, at: square * (LINEAR * wide(g, at) + v))
    product(m0, w, h, lambda v, at: LINEAR * wide(w, at) + v)
    product(h, h, m1, lambda v, at: CUBIC * wide(h, at) + QUINTIC * v)
    product(m1, h, w, lambda v, at: LINEAR * wide(h, at) + v)
    product(m1, w, g, lambda v, at: LINEAR * wide(w, at) + v)
    product(m1, m0, s, lambda v, at: LINEAR * (wide(m0, at) + wide(m1, at)) + v)
    product(g, g, m0, lambda v, at: CUBIC * wide(g, at) + QUINTIC * v)
    product(m0, s, h, lambda v, at: LINEAR * wide(s, at) + LINEAR * LINEAR * wide(m0, at) + v)
    loading.wait()
    for i in range(SIDE):
        value = jnp.dot(h[span(i), :], x_buf[...], preferred_element_type=jnp.float32)
        value = value + LINEAR**3 * x_buf[span(i)].astype(jnp.float32)
        out[span(i)] = (value * factor).astype(jnp.bfloat16)


def update_half(x, own, other):
    n, part = x.shape
    anywhere = pl.BlockSpec(memory_space=pl.ANY)
    square = pltpu.VMEM((n, n), jnp.bfloat16)
    return pl.pallas_call(
        update_kernel,
        out_shape=jax.ShapeDtypeStruct((n, part), jnp.bfloat16),
        in_specs=[
            anywhere,
            pl.BlockSpec(memory_space=pltpu.VMEM),
            pl.BlockSpec(memory_space=pltpu.VMEM),
        ],
        out_specs=pl.BlockSpec(memory_space=pltpu.VMEM),
        scratch_shapes=[
            pltpu.VMEM((n, part), jnp.bfloat16),
            *[square] * 6,
            pltpu.SemaphoreType.DMA,
        ],
        compiler_params=pltpu.CompilerParams(vmem_limit_bytes=40 * MIB),
        cost_estimate=cost(2 * n * n * (9 * n + part), n * part * 4 + n * n * 6),
        name="update",
    )(x, own, other)


def exchange(x):
    return lax.all_to_all(x, "fsdp", split_axis=0, concat_axis=0, tiled=True)


def local(momentum, gradient):
    count = lax.axis_size("fsdp")
    mats, rows, width = momentum.shape
    half = width // 2
    x = exchange(steer_pieces(momentum, gradient)).reshape(count * rows, half)
    new_momentum = 0.95 * momentum + gradient.astype(jnp.float32)
    x, new_momentum = lax.optimization_barrier((x, new_momentum))
    own, sent = gram_half(x)
    other = partner(sent, "fsdp", 0)
    returned = exchange(update_half(x, own, other).reshape(count, rows, half))
    update = returned.reshape(mats, 2, rows, half).transpose(0, 2, 1, 3).reshape(mats, rows, width)
    return (new_momentum, update)


def solution(mesh):
    return jax.shard_map(
        local,
        mesh=mesh,
        in_specs=(P(None, "fsdp", None), P(None, "fsdp", None)),
        out_specs=(P(None, "fsdp", None), P(None, "fsdp", None)),
        check_vma=False,
    )
```

time: 218 us -> 148 us (0.68)
  matrix products: 63.1 us -> 0 us
  blocking collectives: 110 us -> 50.5 us
  Pallas kernels: 0 us -> 31.4 us
  waiting for transfers between devices: 21.8 us -> 41.1 us
  starting transfers between devices: 2.38 us -> 13.5 us
  local copies, waits for them, and re-layouts: 7.78 us -> 1.84 us
  other arithmetic: 11.5 us -> 8.33 us
    dot_general x7 -> x0, matrix products: 63.1 us -> none  [the longest x3 42.1 us: local(): jnp.dot(mix, x, preferred_element_type=jnp.float32)]
    all_to_all x2 -> x1, blocking collectives: 110 us -> 50.5 us  [exchange(): return lax.all_to_all(x, 'fsdp', split_axis=0, concat_axis=0, tiled=True)]
    all_to_all x0 -> x1, waiting for transfers between devices: none -> 38.4 us  [exchange(): return lax.all_to_all(x, 'fsdp', split_axis=0, concat_axis=0, tiled=True)]
    pallas_call x0 -> x3, Pallas kernels: none -> 31.4 us  [the longest x1 19.1 us: update_half(): pl.pallas_call(update_kernel, out_shape=jax.ShapeDtypeStruct((n, part), j...]
    ppermute x4 -> x1, waiting for transfers between devices: 21.8 us -> 2.66 us  [partner(): lax.ppermute(x, axis, [(i, i ^ 1 << apart) for i in range(lax.axis_size(a...]
    all_to_all x0 -> x1, starting transfers between devices: none -> 11.9 us  [exchange(): return lax.all_to_all(x, 'fsdp', split_axis=0, concat_axis=0, tiled=True)]
    convert_element_type x1 -> x0, other arithmetic: 8.72 us -> none  [local(): (gradient.astype(jnp.float32) + 0.95 * new_momentum).astype(jnp.bfloat16)]
    add x0 -> x1, other arithmetic: none -> 8.33 us  [local(): new_momentum = 0.95 * momentum + gradient.astype(jnp.float32)]
  transfers between devices with their start and end apart: 4 -> 2, of which waited for: 4 -> 2; matrix products, arithmetic and copies ran while one was open for 0% -> 6% of each run, Pallas kernels for 0% -> 0%
where the time goes in v1:
time: 148 us; the launch traced here: 147 us
  blocking collectives  50.5 us (34%)
  waiting for transfers between devices  41.1 us (28%)
  Pallas kernels  31.4 us (21%)
  starting transfers between devices  13.5 us (9%)
  other arithmetic  8.33 us (6%)
  local copies, waits for them, and re-layouts  1.84 us (1%)
    all_to_all x1, blocking collectives, exchange(): return lax.all_to_all(x, 'fsdp', split_axis=0, concat_axis=0, tiled=True)  50.5 us
    all_to_all x1, waiting for transfers between devices, exchange(): return lax.all_to_all(x, 'fsdp', split_axis=0, concat_axis=0, tiled=True)  38.4 us
    pallas_call x1, Pallas kernels, update_half(): pl.pallas_call(update_kernel, out_shape=jax.ShapeDtypeStruct((n, part), j...  19.1 us
    all_to_all x1, starting transfers between devices, exchange(): return lax.all_to_all(x, 'fsdp', split_axis=0, concat_axis=0, tiled=True)  11.9 us
    add x1, other arithmetic, local(): new_momentum = 0.95 * momentum + gradient.astype(jnp.float32)  8.33 us
    pallas_call x1, Pallas kernels, gram_half(): pl.pallas_call(gram_kernel, out_shape=(jax.ShapeDtypeStruct(shape, jnp.fl...  6.2 us
    pallas_call x1, Pallas kernels, steer_pieces(): pl.pallas_call(steer_kernel, out_shape=jax.ShapeDtypeStruct(shape, jnp.bf...  6.12 us
  transfers between devices with their start and end apart: 2, of which 2 were waited for; matrix products, arithmetic and copies ran while one was open for 6% of the time, Pallas kernels for 0%

profile of v1, /device:TPU:1, one launch (start us, length us, event | category | flops | bytes accessed | tf_op | source)
XLA Modules:
  0.0 147.3 jit_solution(4342413165544342119)
XLA Ops:
  0.6 6.1 %steer.1 = bf16[64,2,8,1792]{3,2,1,0:T(8,128)(2,1)} custom-call(f32[64,8,3584]{2,1,0:T(8,128)} %momentum.1, bf16[64,8,3584]{2,1,0:T(8,128)(2,1)} %gradient.1), custom_call_target="tpu_custom_call" | custom-call | flops 7340032 | bytes 14680064 | tf_op jit(solution)/shard_map/steer/pallas_call | solution.py:74
  6.8 11.9 %all-to-all-start = ((bf16[128,8,1792]{2,1,0:T(8,128)(2,1)}), bf16[128,8,1792]{2,1,0:T(8,128)(2,1)}, u32[]{:S(2)}, u32[]{:S(2)}) async-start(bf16[128,8,1792]{2,1,0:T(8,128)(2,1)} %bitcast.9), calls=%async_computation | async-start | bytes 7340032 | tf_op jit(solution)/shard_map/all_to_all | solution.py:208
  18.7 8.3 %convert_add_fusion = f32[64,8,3584]{2,1,0:T(8,128)} fusion(bf16[64,8,3584]{2,1,0:T(8,128)(2,1)} %gradient.1, f32[64,8,3584]{2,1,0:T(8,128)} %momentum.1), kind=kLoop, calls=%fused_computation | loop fusion | flops 5505024 | bytes 18350080 | tf_op jit(solution)/shard_map/add | solution.py:216
  27.0 38.4 %all-to-all-done = bf16[128,8,1792]{2,1,0:T(8,128)(2,1)} async-done(((bf16[128,8,1792]{2,1,0:T(8,128)(2,1)}), bf16[128,8,1792]{2,1,0:T(8,128)(2,1)}, u32[]{:S(2)}, u32[]{:S(2)}) %all-to-all-start) | async-done | bytes 3670048 | tf_op jit(solution)/shard_map/all_to_all | solution.py:208
  65.4 6.2 %gram.1 = (f32[2560,256]{1,0:T(8,128)S(1)}, bf16[2560,256]{1,0:T(8,128)(2,1)S(1)}) custom-call(bf16[1024,1792]{1,0:T(8,128)(2,1)} %bitcast.1.x), custom_call_target="tpu_custom_call" | custom-call | flops 2348810240 | bytes 7602176 | tf_op jit(solution)/shard_map/gram/pallas_call | solution.py:115
  71.6 1.6 %collective-permute-start = (bf16[2560,256]{1,0:T(8,128)(2,1)S(1)}, bf16[2560,256]{1,0:T(8,128)(2,1)S(1)}, u32[]{:S(2)}, u32[]{:S(2)}) collective-permute-start(bf16[2560,256]{1,0:T(8,128)(2,1)S(1)} %get-tuple-element.9), channel_id=1, source_target_pairs={{0,1},{1,0},{2,3},{3,2},{4,5},{5,4},{6,7},{7,6},{8,9},{9,8},{10,11... | collective-permute-start | bytes 3932168 | tf_op jit(solution)/shard_map/ppermute | solution.py:28
  73.2 2.7 %collective-permute-done.other = bf16[2560,256]{1,0:T(8,128)(2,1)S(1)} collective-permute-done((bf16[2560,256]{1,0:T(8,128)(2,1)S(1)}, bf16[2560,256]{1,0:T(8,128)(2,1)S(1)}, u32[]{:S(2)}, u32[]{:S(2)}) %collective-permute-start) | collective-permute-done | bytes 1310752 | tf_op jit(solution)/shard_map/ppermute | solution.py:28
  75.9 19.1 %update.1 = bf16[1024,1792]{1,0:T(8,128)(2,1)S(1)} custom-call(bf16[1024,1792]{1,0:T(8,128)(2,1)} %bitcast.1.x, f32[2560,256]{1,0:T(8,128)S(1)} %get-tuple-element.8.own, bf16[2560,256]{1,0:T(8,128)(2,1)S(1)} %collective-permute-done.other), custom_call_target="tpu_custom_call" | custom-call | flops 23085449216 | bytes 13631488 | tf_op jit(solution)/shard_map/update/pallas_call | solution.py:187
  95.0 50.5 %all_to_all.10 = bf16[128,8,1792]{2,1,0:T(8,128)(2,1)S(1)} all-to-all(bf16[128,8,1792]{2,1,0:T(8,128)(2,1)S(1)} %bitcast.8), channel_id=1, replica_groups=mesh['fsdp'=128] {'fsdp'}, dimensions={0} | all-to-all | bytes 7340032 | tf_op jit(solution)/shard_map/all_to_all | solution.py:208
  145.5 1.8 %copy.5 = bf16[64,8,3584]{2,1,0:T(8,128)(2,1)} copy(bf16[64,8,3584]{2,1,0:T(8,128)(2,1)S(1)} %bitcast.10) | data formatting | bytes 7340032
Async XLA Ops:
  6.8 58.7 %all-to-all-start = ((bf16[128,8,1792]{2,1,0:T(8,128)(2,1)}), bf16[128,8,1792]{2,1,0:T(8,128)(2,1)}, u32[]{:S(2)}, u32[]{:S(2)}) async-start(bf16[128,8,1792]{2,1,0:T(8,128)(2,1)} %bitcast.9), calls=%async_computation | async-start | bytes 7340032 | tf_op jit(solution)/shard_map/all_to_all | solution.py:208
  71.6 4.2 %collective-permute-start = (bf16[2560,256]{1,0:T(8,128)(2,1)S(1)}, bf16[2560,256]{1,0:T(8,128)(2,1)S(1)}, u32[]{:S(2)}, u32[]{:S(2)}) collective-permute-start(bf16[2560,256]{1,0:T(8,128)(2,1)S(1)} %get-tuple-element.9), channel_id=1, source_target_pairs={{0,1},{1,0},{2,3},{3,2},{4,5},{5,4},{6,7},{7,6},{8,9},{9,8},{10,11... | collective-permute-start | bytes 3932168 | tf_op jit(solution)/shard_map/ppermute | solution.py:28

commit v2 on v1

--- a/solution.py
+++ b/solution.py
@@ -90,17 +90,11 @@
     )(momentum, gradient).reshape(mats * 2, rows, width // 2)
 
 
-def gram_kernel(x, own, sent, x_buf, sem):
-    arriving = []
-    for i in range(SIDE):
-        copy = pltpu.make_async_copy(x.at[span(i)], x_buf.at[span(i)], sem.at[i])
-        copy.start()
-        arriving.append(copy)
-    for j in range(SIDE):
-        arriving[j].wait()
+def gram_kernel(x, own, sent):
+    for j in reversed(range(SIDE)):
         value = lax.dot_general(
-            x_buf[0 : (j + 1) * TILE],
-            x_buf[span(j)],
+            x[0 : (j + 1) * TILE],
+            x[span(j)],
             (((1,), (1,)), ((), ())),
             preferred_element_type=jnp.float32,
         )
@@ -118,12 +112,8 @@
             jax.ShapeDtypeStruct(shape, jnp.float32),
             jax.ShapeDtypeStruct(shape, jnp.bfloat16),
         ),
-        in_specs=[pl.BlockSpec(memory_space=pl.ANY)],
-        scratch_shapes=[
-            pltpu.VMEM((rows, part), jnp.bfloat16),
-            pltpu.SemaphoreType.DMA((SIDE,)),
-        ],
-        compiler_params=pltpu.CompilerParams(vmem_limit_bytes=32 * MIB),
+        in_specs=[pl.BlockSpec(memory_space=pltpu.VMEM)],
+        compiler_params=pltpu.CompilerParams(vmem_limit_bytes=16 * MIB),
         cost_estimate=cost(2 * len(PAIRS) * TILE * TILE * part, rows * part * 2 + len(PAIRS) * TILE * TILE * 6),
         name="gram",
     )(x)
@@ -152,7 +142,7 @@
     square = inverse * inverse
 
     def product(left, right, store, rest):
-        for j in range(SIDE):
+        for j in reversed(range(SIDE)):
             at = (slice(0, (j + 1) * TILE), span(j))
             value = jnp.dot(left[at[0], :], right[:, at[1]], preferred_element_type=jnp.float32)
             narrow = rest(value, at).astype(jnp.bfloat16)

time: 148 us -> 144 us (0.973)
  Pallas kernels: 31.4 us -> 28.1 us
    pallas_call x1, Pallas kernels: 19.1 us -> 17.4 us  [update_half(): pl.pallas_call(update_kernel, out_shape=jax.ShapeDtypeStruct((n, part), j...]
    pallas_call x1, Pallas kernels: 6.2 us -> 4.6 us  [gram_half(): pl.pallas_call(gram_kernel, out_shape=(jax.ShapeDtypeStruct(shape, jnp.fl...]
where the time goes in v2:
time: 144 us
  blocking collectives  50.5 us (35%)
  waiting for transfers between devices  41.1 us (29%)
  Pallas kernels  28.1 us (20%)
  starting transfers between devices  13.5 us (9%)
  other arithmetic  8.33 us (6%)
  local copies, waits for them, and re-layouts  1.84 us (1%)
    all_to_all x1, blocking collectives, exchange(): return lax.all_to_all(x, 'fsdp', split_axis=0, concat_axis=0, tiled=True)  50.5 us
    all_to_all x1, waiting for transfers between devices, exchange(): return lax.all_to_all(x, 'fsdp', split_axis=0, concat_axis=0, tiled=True)  38.4 us
    pallas_call x1, Pallas kernels, update_half(): pl.pallas_call(update_kernel, out_shape=jax.ShapeDtypeStruct((n, part), j...  17.4 us
    all_to_all x1, starting transfers between devices, exchange(): return lax.all_to_all(x, 'fsdp', split_axis=0, concat_axis=0, tiled=True)  11.9 us
    add x1, other arithmetic, local(): new_momentum = 0.95 * momentum + gradient.astype(jnp.float32)  8.33 us
    pallas_call x1, Pallas kernels, steer_pieces(): pl.pallas_call(steer_kernel, out_shape=jax.ShapeDtypeStruct(shape, jnp.bf...  6.12 us
    pallas_call x1, Pallas kernels, gram_half(): pl.pallas_call(gram_kernel, out_shape=(jax.ShapeDtypeStruct(shape, jnp.fl...  4.6 us
  transfers between devices with their start and end apart: 2, of which 2 were waited for; matrix products, arithmetic and copies ran while one was open for 6% of the time, Pallas kernels for 0%

profile of v2, /device:TPU:1, one launch (start us, length us, event | category | flops | bytes accessed | tf_op | source)
XLA Modules:
  0.0 144.0 jit_solution(4519324796482458114)
XLA Ops:
  0.6 6.1 %steer.1 = bf16[64,2,8,1792]{3,2,1,0:T(8,128)(2,1)} custom-call(f32[64,8,3584]{2,1,0:T(8,128)} %momentum.1, bf16[64,8,3584]{2,1,0:T(8,128)(2,1)} %gradient.1), custom_call_target="tpu_custom_call" | custom-call | flops 7340032 | bytes 14680064 | tf_op jit(solution)/shard_map/steer/pallas_call | solution.py:74
  6.8 11.9 %all-to-all-start = ((bf16[128,8,1792]{2,1,0:T(8,128)(2,1)}), bf16[128,8,1792]{2,1,0:T(8,128)(2,1)}, u32[]{:S(2)}, u32[]{:S(2)}) async-start(bf16[128,8,1792]{2,1,0:T(8,128)(2,1)} %bitcast.9), calls=%async_computation | async-start | bytes 7340032 | tf_op jit(solution)/shard_map/all_to_all | solution.py:198
  18.7 8.3 %convert_add_fusion = f32[64,8,3584]{2,1,0:T(8,128)} fusion(bf16[64,8,3584]{2,1,0:T(8,128)(2,1)} %gradient.1, f32[64,8,3584]{2,1,0:T(8,128)} %momentum.1), kind=kLoop, calls=%fused_computation | loop fusion | flops 5505024 | bytes 18350080 | tf_op jit(solution)/shard_map/add | solution.py:206
  27.0 38.4 %all-to-all-done = bf16[128,8,1792]{2,1,0:T(8,128)(2,1)} async-done(((bf16[128,8,1792]{2,1,0:T(8,128)(2,1)}), bf16[128,8,1792]{2,1,0:T(8,128)(2,1)}, u32[]{:S(2)}, u32[]{:S(2)}) %all-to-all-start) | async-done | bytes 3670048 | tf_op jit(solution)/shard_map/all_to_all | solution.py:198
  65.4 4.6 %gram.1 = (f32[2560,256]{1,0:T(8,128)S(1)}, bf16[2560,256]{1,0:T(8,128)(2,1)S(1)}) custom-call(bf16[1024,1792]{1,0:T(8,128)(2,1)} %bitcast.1.x), custom_call_target="tpu_custom_call" | custom-call | flops 2348810240 | bytes 7602176 | tf_op jit(solution)/shard_map/gram/pallas_call | solution.py:109
  70.0 1.6 %collective-permute-start = (bf16[2560,256]{1,0:T(8,128)(2,1)S(1)}, bf16[2560,256]{1,0:T(8,128)(2,1)S(1)}, u32[]{:S(2)}, u32[]{:S(2)}) collective-permute-start(bf16[2560,256]{1,0:T(8,128)(2,1)S(1)} %get-tuple-element.9), channel_id=1, source_target_pairs={{0,1},{1,0},{2,3},{3,2},{4,5},{5,4},{6,7},{7,6},{8,9},{9,8},{10,11... | collective-permute-start | bytes 3932168 | tf_op jit(solution)/shard_map/ppermute | solution.py:28
  71.6 2.7 %collective-permute-done.other = bf16[2560,256]{1,0:T(8,128)(2,1)S(1)} collective-permute-done((bf16[2560,256]{1,0:T(8,128)(2,1)S(1)}, bf16[2560,256]{1,0:T(8,128)(2,1)S(1)}, u32[]{:S(2)}, u32[]{:S(2)}) %collective-permute-start) | collective-permute-done | bytes 1310752 | tf_op jit(solution)/shard_map/ppermute | solution.py:28
  74.3 17.4 %update.1 = bf16[1024,1792]{1,0:T(8,128)(2,1)S(1)} custom-call(bf16[1024,1792]{1,0:T(8,128)(2,1)} %bitcast.1.x, f32[2560,256]{1,0:T(8,128)S(1)} %get-tuple-element.8.own, bf16[2560,256]{1,0:T(8,128)(2,1)S(1)} %collective-permute-done.other), custom_call_target="tpu_custom_call" | custom-call | flops 23085449216 | bytes 13631488 | tf_op jit(solution)/shard_map/update/pallas_call | solution.py:177
  91.7 50.5 %all_to_all.10 = bf16[128,8,1792]{2,1,0:T(8,128)(2,1)S(1)} all-to-all(bf16[128,8,1792]{2,1,0:T(8,128)(2,1)S(1)} %bitcast.8), channel_id=1, replica_groups=mesh['fsdp'=128] {'fsdp'}, dimensions={0} | all-to-all | bytes 7340032 | tf_op jit(solution)/shard_map/all_to_all | solution.py:198
  142.2 1.8 %copy.5 = bf16[64,8,3584]{2,1,0:T(8,128)(2,1)} copy(bf16[64,8,3584]{2,1,0:T(8,128)(2,1)S(1)} %bitcast.10) | data formatting | bytes 7340032
Async XLA Ops:
  6.8 58.7 %all-to-all-start = ((bf16[128,8,1792]{2,1,0:T(8,128)(2,1)}), bf16[128,8,1792]{2,1,0:T(8,128)(2,1)}, u32[]{:S(2)}, u32[]{:S(2)}) async-start(bf16[128,8,1792]{2,1,0:T(8,128)(2,1)} %bitcast.9), calls=%async_computation | async-start | bytes 7340032 | tf_op jit(solution)/shard_map/all_to_all | solution.py:198
  70.0 4.2 %collective-permute-start = (bf16[2560,256]{1,0:T(8,128)(2,1)S(1)}, bf16[2560,256]{1,0:T(8,128)(2,1)S(1)}, u32[]{:S(2)}, u32[]{:S(2)}) collective-permute-start(bf16[2560,256]{1,0:T(8,128)(2,1)S(1)} %get-tuple-element.9), channel_id=1, source_target_pairs={{0,1},{1,0},{2,3},{3,2},{4,5},{5,4},{6,7},{7,6},{8,9},{9,8},{10,11... | collective-permute-start | bytes 3932168 | tf_op jit(solution)/shard_map/ppermute | solution.py:28

commit v3 on v2

--- a/solution.py
+++ b/solution.py
@@ -29,65 +29,65 @@
 
 
 STEER_PARTS = 8
-
-
-def steer_kernel(momentum, gradient, steer, m_buf, g_buf, s_buf, m_sem, g_sem, s_sem):
-    mats, rows, width = m_buf.shape
+AFTER_PARTS = 4
+
+
+def steer_kernel(momentum, gradient, *rest):
+    afters, (steer, g_buf, m_sem, g_sem) = rest[:AFTER_PARTS], rest[AFTER_PARTS:]
+    mats, rows, width = g_buf.shape
     half = width // 2
     group = mats // STEER_PARTS
+    share = STEER_PARTS // AFTER_PARTS
     arriving = []
     for c in range(STEER_PARTS):
         at = pl.ds(c * group, group)
+        after = afters[c // share].at[pl.ds(c % share * group, group)]
         pair = (
-            pltpu.make_async_copy(momentum.at[at], m_buf.at[at], m_sem.at[c]),
+            pltpu.make_async_copy(momentum.at[at], after, m_sem.at[c]),
             pltpu.make_async_copy(gradient.at[at], g_buf.at[at], g_sem.at[c]),
         )
         for copy in pair:
             copy.start()
         arriving.append(pair)
-    leaving = []
     for c in range(STEER_PARTS):
         for copy in arriving[c]:
             copy.wait()
 
-        @pl.loop(c * group, (c + 1) * group)
-        def _(m):
+        after = afters[c // share]
+
+        @pl.loop(0, group)
+        def _(i):
+            m = c * group + i
+            place = c % share * group + i
             g = g_buf[m].astype(jnp.float32)
-            moved = 0.95 * m_buf[m] + g
+            moved = 0.95 * after[place] + g
+            after[place] = moved
             value = (g + 0.95 * moved).astype(jnp.bfloat16)
-            s_buf[m, 0] = value[:, :half]
-            s_buf[m, 1] = value[:, half:]
-
-        at = pl.ds(c * group, group)
-        copy = pltpu.make_async_copy(s_buf.at[at], steer.at[at], s_sem.at[c])
-        copy.start()
-        leaving.append(copy)
-    for copy in leaving:
-        copy.wait()
+            steer[m, 0] = value[:, :half]
+            steer[m, 1] = value[:, half:]
 
 
 def steer_pieces(momentum, gradient):
     mats, rows, width = momentum.shape
     shape = (mats, 2, rows, width // 2)
     anywhere = pl.BlockSpec(memory_space=pl.ANY)
+    inside = pl.BlockSpec(memory_space=pltpu.VMEM)
     dma = pltpu.SemaphoreType.DMA((STEER_PARTS,))
-    return pl.pallas_call(
+    quarter = jax.ShapeDtypeStruct((mats // AFTER_PARTS, rows, width), jnp.float32)
+    *afters, steer = pl.pallas_call(
         steer_kernel,
-        out_shape=jax.ShapeDtypeStruct(shape, jnp.bfloat16),
+        out_shape=(
+            *[quarter] * AFTER_PARTS,
+            jax.ShapeDtypeStruct(shape, jnp.bfloat16),
+        ),
         in_specs=[anywhere] * 2,
-        out_specs=anywhere,
-        scratch_shapes=[
-            pltpu.VMEM(momentum.shape, jnp.float32),
-            pltpu.VMEM(gradient.shape, jnp.bfloat16),
-            pltpu.VMEM(shape, jnp.bfloat16),
-            dma,
-            dma,
-            dma,
-        ],
-        compiler_params=pltpu.CompilerParams(vmem_limit_bytes=56 * MIB),
+        out_specs=(inside,) * (AFTER_PARTS + 1),
+        scratch_shapes=[pltpu.VMEM(gradient.shape, jnp.bfloat16), dma, dma],
+        compiler_params=pltpu.CompilerParams(vmem_limit_bytes=40 * MIB),
         cost_estimate=cost(4 * momentum.size, 8 * momentum.size),
         name="steer",
-    )(momentum, gradient).reshape(mats * 2, rows, width // 2)
+    )(momentum, gradient)
+    return afters, steer.reshape(mats * 2, rows, width // 2)
 
 
 def gram_kernel(x, own, sent):
@@ -119,10 +119,18 @@
     )(x)
 
 
-def update_kernel(x, own, other, out, x_buf, g, h, s, w, m0, m1, x_sem):
+def update_kernel(x, own, other, *rest):
+    afters = rest[:AFTER_PARTS]
+    out, stored, x_buf, g, h, s, w, m0, m1, x_sem, after_sem = rest[AFTER_PARTS:]
     n, part = x_buf.shape
     loading = pltpu.make_async_copy(x, x_buf, x_sem)
     loading.start()
+    storing = []
+    for c, after in enumerate(afters):
+        share = after.shape[0]
+        copy = pltpu.make_async_copy(after, stored.at[pl.ds(c * share, share)], after_sem.at[c])
+        copy.start()
+        storing.append(copy)
     here = lax.broadcasted_iota(jnp.int32, (TILE, TILE), 0) == lax.broadcasted_iota(
         jnp.int32, (TILE, TILE), 1
     )
@@ -168,30 +176,33 @@
         value = jnp.dot(h[span(i), :], x_buf[...], preferred_element_type=jnp.float32)
         value = value + LINEAR**3 * x_buf[span(i)].astype(jnp.float32)
         out[span(i)] = (value * factor).astype(jnp.bfloat16)
-
-
-def update_half(x, own, other):
+    for copy in storing:
+        copy.wait()
+
+
+def update_half(x, own, other, afters):
     n, part = x.shape
     anywhere = pl.BlockSpec(memory_space=pl.ANY)
+    inside = pl.BlockSpec(memory_space=pltpu.VMEM)
     square = pltpu.VMEM((n, n), jnp.bfloat16)
     return pl.pallas_call(
         update_kernel,
-        out_shape=jax.ShapeDtypeStruct((n, part), jnp.bfloat16),
-        in_specs=[
-            anywhere,
-            pl.BlockSpec(memory_space=pltpu.VMEM),
-            pl.BlockSpec(memory_space=pltpu.VMEM),
-        ],
-        out_specs=pl.BlockSpec(memory_space=pltpu.VMEM),
+        out_shape=(
+            jax.ShapeDtypeStruct((n, part), jnp.bfloat16),
+            jax.ShapeDtypeStruct((afters[0].shape[0] * AFTER_PARTS, *afters[0].shape[1:]), jnp.float32),
+        ),
+        in_specs=[anywhere, inside, inside, *[anywhere] * AFTER_PARTS],
+        out_specs=(inside, anywhere),
         scratch_shapes=[
             pltpu.VMEM((n, part), jnp.bfloat16),
             *[square] * 6,
             pltpu.SemaphoreType.DMA,
+            pltpu.SemaphoreType.DMA((AFTER_PARTS,)),
         ],
-        compiler_params=pltpu.CompilerParams(vmem_limit_bytes=40 * MIB),
+        compiler_params=pltpu.CompilerParams(vmem_limit_bytes=30 * MIB),
         cost_estimate=cost(2 * n * n * (9 * n + part), n * part * 4 + n * n * 6),
         name="update",
-    )(x, own, other)
+    )(x, own, other, *afters)
 
 
 def exchange(x):
@@ -202,12 +213,12 @@
     count = lax.axis_size("fsdp")
     mats, rows, width = momentum.shape
     half = width // 2
-    x = exchange(steer_pieces(momentum, gradient)).reshape(count * rows, half)
-    new_momentum = 0.95 * momentum + gradient.astype(jnp.float32)
-    x, new_momentum = lax.optimization_barrier((x, new_momentum))
+    afters, pieces = steer_pieces(momentum, gradient)
+    x = exchange(pieces).reshape(count * rows, half)
     own, sent = gram_half(x)
     other = partner(sent, "fsdp", 0)
-    returned = exchange(update_half(x, own, other).reshape(count, rows, half))
+    outgoing, new_momentum = update_half(x, own, other, afters)
+    returned = exchange(outgoing.reshape(count, rows, half))
     update = returned.reshape(mats, 2, rows, half).transpose(0, 2, 1, 3).reshape(mats, rows, width)
     return (new_momentum, update)
 

time: 144 us -> 140 us (0.972)
  blocking collectives: 50.5 us -> 109 us
  waiting for transfers between devices: 41.1 us -> 2.66 us
  starting transfers between devices: 13.5 us -> 1.39 us
  other arithmetic: 8.33 us -> 0 us
  Pallas kernels: 28.1 us -> 24.9 us
    all_to_all x1 -> x2, blocking collectives: 50.5 us -> 109 us  [exchange(): return lax.all_to_all(x, 'fsdp', split_axis=0, concat_axis=0, tiled=True)]
    all_to_all x1 -> x0, waiting for transfers between devices: 38.4 us -> none  [exchange(): return lax.all_to_all(x, 'fsdp', split_axis=0, concat_axis=0, tiled=True)]
    all_to_all x1 -> x0, starting transfers between devices: 11.9 us -> none  [exchange(): return lax.all_to_all(x, 'fsdp', split_axis=0, concat_axis=0, tiled=True)]
    add x1 -> x0, other arithmetic: 8.33 us -> none  [local(): new_momentum = 0.95 * momentum + gradient.astype(jnp.float32)]
    pallas_call x1, Pallas kernels: 4.6 us -> 2.56 us  [gram_half(): pl.pallas_call(gram_kernel, out_shape=(jax.ShapeDtypeStruct(shape, jnp.fl...]
  transfers between devices with their start and end apart: 2 -> 1, of which waited for: 2 -> 1; matrix products, arithmetic and copies ran while one was open for 6% -> 0% of each run, Pallas kernels for 0% -> 0%
where the time goes in v3:
time: 140 us
  blocking collectives  109 us (78%)
  Pallas kernels  24.9 us (18%)
  waiting for transfers between devices  2.66 us (2%)
  local copies, waits for them, and re-layouts  1.84 us (1%)
    all_to_all x2, blocking collectives, exchange(): return lax.all_to_all(x, 'fsdp', split_axis=0, concat_axis=0, tiled=True)  109 us
    pallas_call x1, Pallas kernels, update_half(): pl.pallas_call(update_kernel, out_shape=(jax.ShapeDtypeStruct((n, part),...  17.9 us
    pallas_call x1, Pallas kernels, steer_pieces(): pl.pallas_call(steer_kernel, out_shape=(*[quarter] * AFTER_PARTS, jax.Sha...  4.46 us
  transfers between devices with their start and end apart: 1, of which 1 were waited for; matrix products, arithmetic and copies ran while one was open for 0% of the time, Pallas kernels for 0%

profile of v3, /device:TPU:1, one launch (start us, length us, event | category | flops | bytes accessed | tf_op | source)
XLA Modules:
  0.0 140.3 jit_solution(9162223646915751050)
XLA Ops:
  0.6 4.5 %steer.1 = (f32[16,8,3584]{2,1,0:T(8,128)S(1)}, f32[16,8,3584]{2,1,0:T(8,128)S(1)}, f32[16,8,3584]{2,1,0:T(8,128)S(1)}, f32[16,8,3584]{2,1,0:T(8,128)S(1)}, bf16[64,2,8,1792]{3,2,1,0:T(8,128)(2,1)S(1)}) custom-call(f32[64,8,3584]{2,1,0:T(8,128)} %momentum.1, bf16[64,8,3584]{2,1,0:T(8,128)(2,1)} %gradient.1), custom_call_target="tpu_custom_call" | custom-call | flops 7340032 | bytes 14680064 | tf_op jit(solution)/shard_map/steer/pallas_call | solution.py:77
  5.1 58.4 %all_to_all.10 = bf16[128,8,1792]{2,1,0:T(8,128)(2,1)S(1)} all-to-all(bf16[128,8,1792]{2,1,0:T(8,128)(2,1)S(1)} %bitcast.11), channel_id=1, replica_groups=mesh['fsdp'=128] {'fsdp'}, dimensions={0} | all-to-all | bytes 7340032 | tf_op jit(solution)/shard_map/all_to_all | solution.py:209
  63.5 2.6 %gram.1 = (f32[2560,256]{1,0:T(8,128)S(1)}, bf16[2560,256]{1,0:T(8,128)(2,1)S(1)}) custom-call(bf16[1024,1792]{1,0:T(8,128)(2,1)S(1)} %bitcast.8), custom_call_target="tpu_custom_call" | custom-call | flops 2348810240 | bytes 7602176 | tf_op jit(solution)/shard_map/gram/pallas_call | solution.py:109
  66.0 1.4 collective-permute-start
  67.4 2.7 %collective-permute-done.other = bf16[2560,256]{1,0:T(8,128)(2,1)S(1)} collective-permute-done((bf16[2560,256]{1,0:T(8,128)(2,1)S(1)}, bf16[2560,256]{1,0:T(8,128)(2,1)S(1)}, u32[]{:S(2)}, u32[]{:S(2)}) %collective-permute-start) | collective-permute-done | bytes 1310752 | tf_op jit(solution)/shard_map/ppermute | solution.py:28
  70.1 17.9 %update.1 = (bf16[1024,1792]{1,0:T(8,128)(2,1)S(1)}, f32[64,8,3584]{2,1,0:T(8,128)}) custom-call(bf16[1024,1792]{1,0:T(8,128)(2,1)S(1)} %bitcast.9, f32[2560,256]{1,0:T(8,128)S(1)} %get-tuple-element.12.own, bf16[2560,256]{1,0:T(8,128)(2,1)S(1)} %collective-permute-done.other, f32[16,8,3584]{2,1,0:T(8,128)S(1)} %get-tuple-element.14.rest_0_, ...), custom_call_target="tpu_custom_call" | custom-call | flops 23085449216 | bytes 13631488 | tf_op jit(solution)/shard_map/update/pallas_call | solution.py:188
  88.0 50.5 %all_to_all.11 = bf16[128,8,1792]{2,1,0:T(8,128)(2,1)S(1)} all-to-all(bf16[128,8,1792]{2,1,0:T(8,128)(2,1)S(1)} %bitcast.10), channel_id=1, replica_groups=mesh['fsdp'=128] {'fsdp'}, dimensions={0} | all-to-all | bytes 7340032 | tf_op jit(solution)/shard_map/all_to_all | solution.py:209
  138.5 1.8 %copy.5 = bf16[64,8,3584]{2,1,0:T(8,128)(2,1)} copy(bf16[64,8,3584]{2,1,0:T(8,128)(2,1)S(1)} %bitcast.12) | data formatting | bytes 7340032
Async XLA Ops:
  66.0 4.1 %collective-permute-start = (bf16[2560,256]{1,0:T(8,128)(2,1)S(1)}, bf16[2560,256]{1,0:T(8,128)(2,1)S(1)}, u32[]{:S(2)}, u32[]{:S(2)}) collective-permute-start(bf16[2560,256]{1,0:T(8,128)(2,1)S(1)} %get-tuple-element.13), channel_id=1, source_target_pairs={{0,1},{1,0},{2,3},{3,2},{4,5},{5,4},{6,7},{7,6},{8,9},{9,8},{10,11... | collective-permute-start | bytes 3932168 | tf_op jit(solution)/shard_map/ppermute | solution.py:28

commit v4 on v3

--- a/solution.py
+++ b/solution.py
@@ -121,10 +121,7 @@
 
 def update_kernel(x, own, other, *rest):
     afters = rest[:AFTER_PARTS]
-    out, stored, x_buf, g, h, s, w, m0, m1, x_sem, after_sem = rest[AFTER_PARTS:]
-    n, part = x_buf.shape
-    loading = pltpu.make_async_copy(x, x_buf, x_sem)
-    loading.start()
+    out, stored, g, h, s, w, m0, m1, after_sem = rest[AFTER_PARTS:]
     storing = []
     for c, after in enumerate(afters):
         share = after.shape[0]
@@ -147,6 +144,7 @@
             g[span(j), span(i)] = narrow.T
     inverse = 1.0 / (jnp.sqrt(total) + 1e-07)
     factor = inverse * FACTOR
+    direct = LINEAR**3 * factor
     square = inverse * inverse
 
     def product(left, right, store, rest):
@@ -170,12 +168,12 @@
     product(m1, w, g, lambda v, at: LINEAR * wide(w, at) + v)
     product(m1, m0, s, lambda v, at: LINEAR * (wide(m0, at) + wide(m1, at)) + v)
     product(g, g, m0, lambda v, at: CUBIC * wide(g, at) + QUINTIC * v)
-    product(m0, s, h, lambda v, at: LINEAR * wide(s, at) + LINEAR * LINEAR * wide(m0, at) + v)
-    loading.wait()
-    for i in range(SIDE):
-        value = jnp.dot(h[span(i), :], x_buf[...], preferred_element_type=jnp.float32)
-        value = value + LINEAR**3 * x_buf[span(i)].astype(jnp.float32)
-        out[span(i)] = (value * factor).astype(jnp.bfloat16)
+    product(
+        m0, s, h, lambda v, at: factor * (LINEAR * wide(s, at) + LINEAR * LINEAR * wide(m0, at) + v)
+    )
+    for i in reversed(range(SIDE)):
+        value = jnp.dot(h[span(i), :], x[...], preferred_element_type=jnp.float32)
+        out[span(i)] = (value + direct * x[span(i)].astype(jnp.float32)).astype(jnp.bfloat16)
     for copy in storing:
         copy.wait()
 
@@ -191,12 +189,10 @@
             jax.ShapeDtypeStruct((n, part), jnp.bfloat16),
             jax.ShapeDtypeStruct((afters[0].shape[0] * AFTER_PARTS, *afters[0].shape[1:]), jnp.float32),
         ),
-        in_specs=[anywhere, inside, inside, *[anywhere] * AFTER_PARTS],
+        in_specs=[inside, inside, inside, *[anywhere] * AFTER_PARTS],
         out_specs=(inside, anywhere),
         scratch_shapes=[
-            pltpu.VMEM((n, part), jnp.bfloat16),
             *[square] * 6,
-            pltpu.SemaphoreType.DMA,
             pltpu.SemaphoreType.DMA((AFTER_PARTS,)),
         ],
         compiler_params=pltpu.CompilerParams(vmem_limit_bytes=30 * MIB),

time: 140 us -> 140 us (level)
  no operation moved by 1% of the time
where the time goes in v4:
time: 140 us; the launch traced here: 139 us
  blocking collectives  109 us (78%)
  Pallas kernels  23.9 us (17%)
  waiting for transfers between devices  2.66 us (2%)
  local copies, waits for them, and re-layouts  1.84 us (1%)
  starting transfers between devices  1.57 us (1%)
    all_to_all x2, blocking collectives, exchange(): return lax.all_to_all(x, 'fsdp', split_axis=0, concat_axis=0, tiled=True)  109 us
    pallas_call x1, Pallas kernels, update_half(): pl.pallas_call(update_kernel, out_shape=(jax.ShapeDtypeStruct((n, part),...  16.8 us
    pallas_call x1, Pallas kernels, steer_pieces(): pl.pallas_call(steer_kernel, out_shape=(*[quarter] * AFTER_PARTS, jax.Sha...  4.46 us
  transfers between devices with their start and end apart: 1, of which 1 were waited for; matrix products, arithmetic and copies ran while one was open for 0% of the time, Pallas kernels for 0%

profile of v4, /device:TPU:1, one launch (start us, length us, event | category | flops | bytes accessed | tf_op | source)
XLA Modules:
  0.0 139.4 jit_solution(9519299119960524395)
XLA Ops:
  0.6 4.5 %steer.1 = (f32[16,8,3584]{2,1,0:T(8,128)S(1)}, f32[16,8,3584]{2,1,0:T(8,128)S(1)}, f32[16,8,3584]{2,1,0:T(8,128)S(1)}, f32[16,8,3584]{2,1,0:T(8,128)S(1)}, bf16[64,2,8,1792]{3,2,1,0:T(8,128)(2,1)S(1)}) custom-call(f32[64,8,3584]{2,1,0:T(8,128)} %momentum.1, bf16[64,8,3584]{2,1,0:T(8,128)(2,1)} %gradient.1), custom_call_target="tpu_custom_call" | custom-call | flops 7340032 | bytes 14680064 | tf_op jit(solution)/shard_map/steer/pallas_call | solution.py:77
  5.1 58.4 %all_to_all.10 = bf16[128,8,1792]{2,1,0:T(8,128)(2,1)S(1)} all-to-all(bf16[128,8,1792]{2,1,0:T(8,128)(2,1)S(1)} %bitcast.11), channel_id=1, replica_groups=mesh['fsdp'=128] {'fsdp'}, dimensions={0} | all-to-all | bytes 7340032 | tf_op jit(solution)/shard_map/all_to_all | solution.py:205
  63.5 2.6 %gram.1 = (f32[2560,256]{1,0:T(8,128)S(1)}, bf16[2560,256]{1,0:T(8,128)(2,1)S(1)}) custom-call(bf16[1024,1792]{1,0:T(8,128)(2,1)S(1)} %bitcast.8), custom_call_target="tpu_custom_call" | custom-call | flops 2348810240 | bytes 7602176 | tf_op jit(solution)/shard_map/gram/pallas_call | solution.py:109
  66.0 1.6 %collective-permute-start = (bf16[2560,256]{1,0:T(8,128)(2,1)S(1)}, bf16[2560,256]{1,0:T(8,128)(2,1)S(1)}, u32[]{:S(2)}, u32[]{:S(2)}) collective-permute-start(bf16[2560,256]{1,0:T(8,128)(2,1)S(1)} %get-tuple-element.13), channel_id=1, source_target_pairs={{0,1},{1,0},{2,3},{3,2},{4,5},{5,4},{6,7},{7,6},{8,9},{9,8},{10,11... | collective-permute-start | bytes 3932168 | tf_op jit(solution)/shard_map/ppermute | solution.py:28
  67.6 2.7 %collective-permute-done.other = bf16[2560,256]{1,0:T(8,128)(2,1)S(1)} collective-permute-done((bf16[2560,256]{1,0:T(8,128)(2,1)S(1)}, bf16[2560,256]{1,0:T(8,128)(2,1)S(1)}, u32[]{:S(2)}, u32[]{:S(2)}) %collective-permute-start) | collective-permute-done | bytes 1310752 | tf_op jit(solution)/shard_map/ppermute | solution.py:28
  70.3 16.8 %update.1 = (bf16[1024,1792]{1,0:T(8,128)(2,1)S(1)}, f32[64,8,3584]{2,1,0:T(8,128)}) custom-call(bf16[1024,1792]{1,0:T(8,128)(2,1)S(1)} %bitcast.9, f32[2560,256]{1,0:T(8,128)S(1)} %get-tuple-element.12.own, bf16[2560,256]{1,0:T(8,128)(2,1)S(1)} %collective-permute-done.other, f32[16,8,3584]{2,1,0:T(8,128)S(1)} %get-tuple-element.14.rest_0_, ...), custom_call_target="tpu_custom_call" | custom-call | flops 23085449216 | bytes 13631488 | tf_op jit(solution)/shard_map/update/pallas_call | solution.py:186
  87.1 50.5 %all_to_all.11 = bf16[128,8,1792]{2,1,0:T(8,128)(2,1)S(1)} all-to-all(bf16[128,8,1792]{2,1,0:T(8,128)(2,1)S(1)} %bitcast.10), channel_id=1, replica_groups=mesh['fsdp'=128] {'fsdp'}, dimensions={0} | all-to-all | bytes 7340032 | tf_op jit(solution)/shard_map/all_to_all | solution.py:205
  137.6 1.8 %copy.5 = bf16[64,8,3584]{2,1,0:T(8,128)(2,1)} copy(bf16[64,8,3584]{2,1,0:T(8,128)(2,1)S(1)} %bitcast.12) | data formatting | bytes 7340032
Async XLA Ops:
  66.0 4.2 %collective-permute-start = (bf16[2560,256]{1,0:T(8,128)(2,1)S(1)}, bf16[2560,256]{1,0:T(8,128)(2,1)S(1)}, u32[]{:S(2)}, u32[]{:S(2)}) collective-permute-start(bf16[2560,256]{1,0:T(8,128)(2,1)S(1)} %get-tuple-element.13), channel_id=1, source_target_pairs={{0,1},{1,0},{2,3},{3,2},{4,5},{5,4},{6,7},{7,6},{8,9},{9,8},{10,11... | collective-permute-start | bytes 3932168 | tf_op jit(solution)/shard_map/ppermute | solution.py:28

commit v5 on v4

--- a/solution.py
+++ b/solution.py
@@ -1,3 +1,5 @@
+import functools
+
 import jax
 import jax.numpy as jnp
 from jax import lax
@@ -12,7 +14,8 @@
 FACTOR = 0.2 * max(FF, D) ** 0.5
 TILE = 256
 SIDE = FF // TILE
-PAIRS = [(i, j) for j in range(SIDE) for i in range(j + 1)]
+GROUPS = [(2, 1, 0), (3,)]
+PAIRS = [[(i, j) for j in group for i in range(j + 1)] for group in GROUPS]
 MIB = 2**20
 
 
@@ -90,36 +93,39 @@
     return afters, steer.reshape(mats * 2, rows, width // 2)
 
 
-def gram_kernel(x, own, sent):
-    for j in reversed(range(SIDE)):
+def gram_kernel(group, x, own, sent):
+    start = 0
+    for j in group:
         value = lax.dot_general(
             x[0 : (j + 1) * TILE],
             x[span(j)],
             (((1,), (1,)), ((), ())),
             preferred_element_type=jnp.float32,
         )
-        at = slice(j * (j + 1) // 2 * TILE, (j + 1) * (j + 2) // 2 * TILE)
+        at = slice(start, start + (j + 1) * TILE)
+        start += (j + 1) * TILE
         own[at] = value
         sent[at] = value.astype(jnp.bfloat16)
 
 
-def gram_half(x):
+def gram_half(x, group, pairs):
     rows, part = x.shape
-    shape = (len(PAIRS) * TILE, TILE)
+    shape = (len(pairs) * TILE, TILE)
     return pl.pallas_call(
-        gram_kernel,
+        functools.partial(gram_kernel, group),
         out_shape=(
             jax.ShapeDtypeStruct(shape, jnp.float32),
             jax.ShapeDtypeStruct(shape, jnp.bfloat16),
         ),
         in_specs=[pl.BlockSpec(memory_space=pltpu.VMEM)],
         compiler_params=pltpu.CompilerParams(vmem_limit_bytes=16 * MIB),
-        cost_estimate=cost(2 * len(PAIRS) * TILE * TILE * part, rows * part * 2 + len(PAIRS) * TILE * TILE * 6),
+        cost_estimate=cost(2 * len(pairs) * TILE * TILE * part, rows * part * 2 + len(pairs) * TILE * TILE * 6),
         name="gram",
     )(x)
 
 
-def update_kernel(x, own, other, *rest):
+def update_kernel(x, *rest):
+    owns, others, rest = rest[: len(GROUPS)], rest[len(GROUPS) : 2 * len(GROUPS)], rest[2 * len(GROUPS) :]
     afters = rest[:AFTER_PARTS]
     out, stored, g, h, s, w, m0, m1, after_sem = rest[AFTER_PARTS:]
     storing = []
@@ -132,16 +138,17 @@
         jnp.int32, (TILE, TILE), 1
     )
     total = jnp.zeros((1, 1), jnp.float32)
-    for k, (i, j) in enumerate(PAIRS):
-        block = own[span(k)] + other[span(k)].astype(jnp.float32)
-        narrow = block.astype(jnp.bfloat16)
-        g[span(i), span(j)] = narrow
-        if i == j:
-            block = jnp.where(here, block, 0.0)
-            block = jnp.sum(block, axis=0, keepdims=True)
-            total = total + jnp.sum(block, axis=1, keepdims=True)
-        else:
-            g[span(j), span(i)] = narrow.T
+    for own, other, pairs in zip(owns, others, PAIRS):
+        for k, (i, j) in enumerate(pairs):
+            block = own[span(k)] + other[span(k)].astype(jnp.float32)
+            narrow = block.astype(jnp.bfloat16)
+            g[span(i), span(j)] = narrow
+            if i == j:
+                block = jnp.where(here, block, 0.0)
+                block = jnp.sum(block, axis=0, keepdims=True)
+                total = total + jnp.sum(block, axis=1, keepdims=True)
+            else:
+                g[span(j), span(i)] = narrow.T
     inverse = 1.0 / (jnp.sqrt(total) + 1e-07)
     factor = inverse * FACTOR
     direct = LINEAR**3 * factor
@@ -178,7 +185,7 @@
         copy.wait()
 
 
-def update_half(x, own, other, afters):
+def update_half(x, owns, others, afters):
     n, part = x.shape
     anywhere = pl.BlockSpec(memory_space=pl.ANY)
     inside = pl.BlockSpec(memory_space=pltpu.VMEM)
@@ -189,7 +196,7 @@
             jax.ShapeDtypeStruct((n, part), jnp.bfloat16),
             jax.ShapeDtypeStruct((afters[0].shape[0] * AFTER_PARTS, *afters[0].shape[1:]), jnp.float32),
         ),
-        in_specs=[inside, inside, inside, *[anywhere] * AFTER_PARTS],
+        in_specs=[inside, *[inside] * (2 * len(GROUPS)), *[anywhere] * AFTER_PARTS],
         out_specs=(inside, anywhere),
         scratch_shapes=[
             *[square] * 6,
@@ -198,7 +205,7 @@
         compiler_params=pltpu.CompilerParams(vmem_limit_bytes=30 * MIB),
         cost_estimate=cost(2 * n * n * (9 * n + part), n * part * 4 + n * n * 6),
         name="update",
-    )(x, own, other, *afters)
+    )(x, *owns, *others, *afters)
 
 
 def exchange(x):
@@ -211,9 +218,12 @@
     half = width // 2
     afters, pieces = steer_pieces(momentum, gradient)
     x = exchange(pieces).reshape(count * rows, half)
-    own, sent = gram_half(x)
-    other = partner(sent, "fsdp", 0)
-    outgoing, new_momentum = update_half(x, own, other, afters)
+    owns, others = [], []
+    for group, pairs in zip(GROUPS, PAIRS):
+        own, sent = gram_half(x, group, pairs)
+        owns.append(own)
+        others.append(partner(sent, "fsdp", 0))
+    outgoing, new_momentum = update_half(x, owns, others, afters)
     returned = exchange(outgoing.reshape(count, rows, half))
     update = returned.reshape(mats, 2, rows, half).transpose(0, 2, 1, 3).reshape(mats, rows, width)
     return (new_momentum, update)

time: 140 us -> 139 us (level)
  transfers between devices with their start and end apart: 1 -> 2, of which waited for: 1 -> 1; matrix products, arithmetic and copies ran while one was open for 0% -> 0% of each run, Pallas kernels for 0% -> 1%
where the time goes in v5:
time: 139 us
  blocking collectives  109 us (78%)
  Pallas kernels  24.1 us (17%)
  waiting for transfers between devices  1.9 us (1%)
  local copies, waits for them, and re-layouts  1.84 us (1%)
  starting transfers between devices  1.67 us (1%)
    all_to_all x2, blocking collectives, exchange(): return lax.all_to_all(x, 'fsdp', split_axis=0, concat_axis=0, tiled=True)  109 us
    pallas_call x1, Pallas kernels, update_half(): pl.pallas_call(update_kernel, out_shape=(jax.ShapeDtypeStruct((n, part),...  16.9 us
    pallas_call x1, Pallas kernels, steer_pieces(): pl.pallas_call(steer_kernel, out_shape=(*[quarter] * AFTER_PARTS, jax.Sha...  4.46 us
  transfers between devices with their start and end apart: 2, of which 1 were waited for; matrix products, arithmetic and copies ran while one was open for 0% of the time, Pallas kernels for 1%

profile of v5, /device:TPU:1, one launch (start us, length us, event | category | flops | bytes accessed | tf_op | source)
XLA Modules:
  0.0 138.8 jit_solution(8550539057744723985)
XLA Ops:
  0.6 4.5 %steer.1 = (f32[16,8,3584]{2,1,0:T(8,128)S(1)}, f32[16,8,3584]{2,1,0:T(8,128)S(1)}, f32[16,8,3584]{2,1,0:T(8,128)S(1)}, f32[16,8,3584]{2,1,0:T(8,128)S(1)}, bf16[64,2,8,1792]{3,2,1,0:T(8,128)(2,1)S(1)}) custom-call(f32[64,8,3584]{2,1,0:T(8,128)} %momentum.1, bf16[64,8,3584]{2,1,0:T(8,128)(2,1)} %gradient.1), custom_call_target="tpu_custom_call" | custom-call | flops 7340032 | bytes 14680064 | tf_op jit(solution)/shard_map/steer/pallas_call | solution.py:80
  5.1 58.4 %all_to_all.10 = bf16[128,8,1792]{2,1,0:T(8,128)(2,1)S(1)} all-to-all(bf16[128,8,1792]{2,1,0:T(8,128)(2,1)S(1)} %bitcast.12), channel_id=1, replica_groups=mesh['fsdp'=128] {'fsdp'}, dimensions={0} | all-to-all | bytes 7340032 | tf_op jit(solution)/shard_map/all_to_all | solution.py:212
  63.5 1.6 %gram.2 = (f32[1536,256]{1,0:T(8,128)S(1)}, bf16[1536,256]{1,0:T(8,128)(2,1)S(1)}) custom-call(bf16[1024,1792]{1,0:T(8,128)(2,1)S(1)} %bitcast.8), custom_call_target="tpu_custom_call" | custom-call | flops 1409286144 | bytes 6029312 | tf_op jit(solution)/shard_map/gram/pallas_call | solution.py:114
  65.1 1.4 %collective-permute-start = (bf16[1536,256]{1,0:T(8,128)(2,1)S(1)}, bf16[1536,256]{1,0:T(8,128)(2,1)S(1)}, u32[]{:S(2)}, u32[]{:S(2)}) collective-permute-start(bf16[1536,256]{1,0:T(8,128)(2,1)S(1)} %get-tuple-element.16), channel_id=1, source_target_pairs={{0,1},{1,0},{2,3},{3,2},{4,5},{5,4},{6,7},{7,6},{8,9},{9,8},{10,11... | collective-permute-start | bytes 2359304 | tf_op jit(solution)/shard_map/ppermute | solution.py:31
  66.5 1.1 gram.3
  67.6 0.3 collective-permute-start.1
  67.9 1.9 %collective-permute-done.1.rest_3_ = bf16[1024,256]{1,0:T(8,128)(2,1)S(1)} collective-permute-done((bf16[1024,256]{1,0:T(8,128)(2,1)S(1)}, bf16[1024,256]{1,0:T(8,128)(2,1)S(1)}, u32[]{:S(2)}, u32[]{:S(2)}) %collective-permute-start.1) | collective-permute-done | bytes 524320 | tf_op jit(solution)/shard_map/ppermute | solution.py:31
  69.8 0.0 collective-permute-done.rest_2_
  69.8 16.9 %update.1 = (bf16[1024,1792]{1,0:T(8,128)(2,1)S(1)}, f32[64,8,3584]{2,1,0:T(8,128)}) custom-call(bf16[1024,1792]{1,0:T(8,128)(2,1)S(1)} %bitcast.10, f32[1536,256]{1,0:T(8,128)S(1)} %get-tuple-element.14.rest_0_, f32[1024,256]{1,0:T(8,128)S(1)} %get-tuple-element.15.rest_1_, bf16[1536,256]{1,0:T(8,128)(2,1)S(1)} %collective-permute-done.rest_2_, ...), custom_call_target="tpu_custom_call" | custom-call | flops 23085449216 | bytes 13631488 | tf_op jit(solution)/shard_map/update/pallas_call | solution.py:193
  86.7 50.3 %all_to_all.11 = bf16[128,8,1792]{2,1,0:T(8,128)(2,1)S(1)} all-to-all(bf16[128,8,1792]{2,1,0:T(8,128)(2,1)S(1)} %bitcast.11), channel_id=1, replica_groups=mesh['fsdp'=128] {'fsdp'}, dimensions={0} | all-to-all | bytes 7340032 | tf_op jit(solution)/shard_map/all_to_all | solution.py:212
  137.0 1.8 %copy.5 = bf16[64,8,3584]{2,1,0:T(8,128)(2,1)} copy(bf16[64,8,3584]{2,1,0:T(8,128)(2,1)S(1)} %bitcast.13) | data formatting | bytes 7340032
Async XLA Ops:
  65.1 4.7 %collective-permute-start = (bf16[1536,256]{1,0:T(8,128)(2,1)S(1)}, bf16[1536,256]{1,0:T(8,128)(2,1)S(1)}, u32[]{:S(2)}, u32[]{:S(2)}) collective-permute-start(bf16[1536,256]{1,0:T(8,128)(2,1)S(1)} %get-tuple-element.16), channel_id=1, source_target_pairs={{0,1},{1,0},{2,3},{3,2},{4,5},{5,4},{6,7},{7,6},{8,9},{9,8},{10,11... | collective-permute-start | bytes 2359304 | tf_op jit(solution)/shard_map/ppermute | solution.py:31
  67.6 2.2 %collective-permute-start.1 = (bf16[1024,256]{1,0:T(8,128)(2,1)S(1)}, bf16[1024,256]{1,0:T(8,128)(2,1)S(1)}, u32[]{:S(2)}, u32[]{:S(2)}) collective-permute-start(bf16[1024,256]{1,0:T(8,128)(2,1)S(1)} %get-tuple-element.17), channel_id=1, source_target_pairs={{0,1},{1,0},{2,3},{3,2},{4,5},{5,4},{6,7},{7,6},{8,9},{9,8},{10,11... | collective-permute-start | bytes 1572872 | tf_op jit(solution)/shard_map/ppermute | solution.py:31

commit v6 on v5

--- a/solution.py
+++ b/solution.py
@@ -155,32 +155,43 @@
     square = inverse * inverse
 
     def product(left, right, store, rest):
+        lost = [None] * SIDE
         for j in reversed(range(SIDE)):
             at = (slice(0, (j + 1) * TILE), span(j))
             value = jnp.dot(left[at[0], :], right[:, at[1]], preferred_element_type=jnp.float32)
-            narrow = rest(value, at).astype(jnp.bfloat16)
+            value = rest(value, at, j)
+            narrow = value.astype(jnp.bfloat16)
             store[at] = narrow
             for i in range(j):
                 store[span(j), span(i)] = narrow[span(i)].T
+            lost[j] = jnp.where(here, value[span(j)] - narrow[span(j)].astype(jnp.float32), 0.0)
+        return lost
 
     def wide(ref, at):
         return ref[at].astype(jnp.float32)
 
 
-    product(g, g, m0, lambda v, at: square * (CUBIC * wide(g, at) + square * (QUINTIC * v)))
-    product(m0, g, w, lambda v, at: square * (LINEAR * wide(g, at) + v))
-    product(m0, w, h, lambda v, at: LINEAR * wide(w, at) + v)
-    product(h, h, m1, lambda v, at: CUBIC * wide(h, at) + QUINTIC * v)
-    product(m1, h, w, lambda v, at: LINEAR * wide(h, at) + v)
-    product(m1, w, g, lambda v, at: LINEAR * wide(w, at) + v)
-    product(m1, m0, s, lambda v, at: LINEAR * (wide(m0, at) + wide(m1, at)) + v)
-    product(g, g, m0, lambda v, at: CUBIC * wide(g, at) + QUINTIC * v)
-    product(
-        m0, s, h, lambda v, at: factor * (LINEAR * wide(s, at) + LINEAR * LINEAR * wide(m0, at) + v)
+    product(g, g, m0, lambda v, at, j: square * (CUBIC * wide(g, at) + square * (QUINTIC * v)))
+    product(m0, g, w, lambda v, at, j: square * (LINEAR * wide(g, at) + v))
+    product(m0, w, h, lambda v, at, j: LINEAR * wide(w, at) + v)
+    product(h, h, m1, lambda v, at, j: CUBIC * wide(h, at) + QUINTIC * v)
+    product(m1, h, w, lambda v, at, j: LINEAR * wide(h, at) + v)
+    product(m1, w, g, lambda v, at, j: LINEAR * wide(w, at) + v)
+    lost = product(m1, m0, s, lambda v, at, j: LINEAR * (wide(m0, at) + wide(m1, at)) + v)
+    across = [jnp.sum(block, axis=0, keepdims=True) for block in lost]
+    down = [LINEAR * jnp.sum(block, axis=1, keepdims=True) for block in lost]
+    product(g, g, m0, lambda v, at, j: CUBIC * wide(g, at) + QUINTIC * v)
+    lost = product(
+        m0,
+        s,
+        h,
+        lambda v, at, j: factor
+        * (LINEAR * wide(s, at) + (LINEAR * LINEAR + across[j]) * wide(m0, at) + v),
     )
     for i in reversed(range(SIDE)):
         value = jnp.dot(h[span(i), :], x[...], preferred_element_type=jnp.float32)
-        out[span(i)] = (value + direct * x[span(i)].astype(jnp.float32)).astype(jnp.bfloat16)
+        diagonal = direct + factor * down[i] + jnp.sum(lost[i], axis=1, keepdims=True)
+        out[span(i)] = (value + diagonal * x[span(i)].astype(jnp.float32)).astype(jnp.bfloat16)
     for copy in storing:
         copy.wait()
 

time: 139 us -> 139 us (level)
  no operation moved by 1% of the time
where the time goes in v6:
time: 139 us
  blocking collectives  109 us (78%)
  Pallas kernels  24.4 us (18%)
  waiting for transfers between devices  1.9 us (1%)
  local copies, waits for them, and re-layouts  1.84 us (1%)
  starting transfers between devices  1.67 us (1%)
    all_to_all x2, blocking collectives, exchange(): return lax.all_to_all(x, 'fsdp', split_axis=0, concat_axis=0, tiled=True)  109 us
    pallas_call x1, Pallas kernels, update_half(): pl.pallas_call(update_kernel, out_shape=(jax.ShapeDtypeStruct((n, part),...  17.2 us
    pallas_call x1, Pallas kernels, steer_pieces(): pl.pallas_call(steer_kernel, out_shape=(*[quarter] * AFTER_PARTS, jax.Sha...  4.46 us
  transfers between devices with their start and end apart: 2, of which 1 were waited for; matrix products, arithmetic and copies ran while one was open for 0% of the time, Pallas kernels for 1%

profile of v6, /device:TPU:1, one launch (start us, length us, event | category | flops | bytes accessed | tf_op | source)
XLA Modules:
  0.0 139.1 jit_solution(1636750713457967235)
XLA Ops:
  0.6 4.5 %steer.1 = (f32[16,8,3584]{2,1,0:T(8,128)S(1)}, f32[16,8,3584]{2,1,0:T(8,128)S(1)}, f32[16,8,3584]{2,1,0:T(8,128)S(1)}, f32[16,8,3584]{2,1,0:T(8,128)S(1)}, bf16[64,2,8,1792]{3,2,1,0:T(8,128)(2,1)S(1)}) custom-call(f32[64,8,3584]{2,1,0:T(8,128)} %momentum.1, bf16[64,8,3584]{2,1,0:T(8,128)(2,1)} %gradient.1), custom_call_target="tpu_custom_call" | custom-call | flops 7340032 | bytes 14680064 | tf_op jit(solution)/shard_map/steer/pallas_call | solution.py:80
  5.1 58.4 %all_to_all.10 = bf16[128,8,1792]{2,1,0:T(8,128)(2,1)S(1)} all-to-all(bf16[128,8,1792]{2,1,0:T(8,128)(2,1)S(1)} %bitcast.12), channel_id=1, replica_groups=mesh['fsdp'=128] {'fsdp'}, dimensions={0} | all-to-all | bytes 7340032 | tf_op jit(solution)/shard_map/all_to_all | solution.py:223
  63.5 1.6 %gram.2 = (f32[1536,256]{1,0:T(8,128)S(1)}, bf16[1536,256]{1,0:T(8,128)(2,1)S(1)}) custom-call(bf16[1024,1792]{1,0:T(8,128)(2,1)S(1)} %bitcast.8), custom_call_target="tpu_custom_call" | custom-call | flops 1409286144 | bytes 6029312 | tf_op jit(solution)/shard_map/gram/pallas_call | solution.py:114
  65.1 1.4 %collective-permute-start = (bf16[1536,256]{1,0:T(8,128)(2,1)S(1)}, bf16[1536,256]{1,0:T(8,128)(2,1)S(1)}, u32[]{:S(2)}, u32[]{:S(2)}) collective-permute-start(bf16[1536,256]{1,0:T(8,128)(2,1)S(1)} %get-tuple-element.16), channel_id=1, source_target_pairs={{0,1},{1,0},{2,3},{3,2},{4,5},{5,4},{6,7},{7,6},{8,9},{9,8},{10,11... | collective-permute-start | bytes 2359304 | tf_op jit(solution)/shard_map/ppermute | solution.py:31
  66.5 1.1 gram.3
  67.6 0.3 collective-permute-start.1
  67.9 1.9 %collective-permute-done.1.rest_3_ = bf16[1024,256]{1,0:T(8,128)(2,1)S(1)} collective-permute-done((bf16[1024,256]{1,0:T(8,128)(2,1)S(1)}, bf16[1024,256]{1,0:T(8,128)(2,1)S(1)}, u32[]{:S(2)}, u32[]{:S(2)}) %collective-permute-start.1) | collective-permute-done | bytes 524320 | tf_op jit(solution)/shard_map/ppermute | solution.py:31
  69.8 0.0 collective-permute-done.rest_2_
  69.8 17.2 %update.1 = (bf16[1024,1792]{1,0:T(8,128)(2,1)S(1)}, f32[64,8,3584]{2,1,0:T(8,128)}) custom-call(bf16[1024,1792]{1,0:T(8,128)(2,1)S(1)} %bitcast.10, f32[1536,256]{1,0:T(8,128)S(1)} %get-tuple-element.14.rest_0_, f32[1024,256]{1,0:T(8,128)S(1)} %get-tuple-element.15.rest_1_, bf16[1536,256]{1,0:T(8,128)(2,1)S(1)} %collective-permute-done.rest_2_, ...), custom_call_target="tpu_custom_call" | custom-call | flops 23085449216 | bytes 13631488 | tf_op jit(solution)/shard_map/update/pallas_call | solution.py:204
  87.0 50.3 %all_to_all.11 = bf16[128,8,1792]{2,1,0:T(8,128)(2,1)S(1)} all-to-all(bf16[128,8,1792]{2,1,0:T(8,128)(2,1)S(1)} %bitcast.11), channel_id=1, replica_groups=mesh['fsdp'=128] {'fsdp'}, dimensions={0} | all-to-all | bytes 7340032 | tf_op jit(solution)/shard_map/all_to_all | solution.py:223
  137.3 1.8 %copy.5 = bf16[64,8,3584]{2,1,0:T(8,128)(2,1)} copy(bf16[64,8,3584]{2,1,0:T(8,128)(2,1)S(1)} %bitcast.13) | data formatting | bytes 7340032
Async XLA Ops:
  65.1 4.7 %collective-permute-start = (bf16[1536,256]{1,0:T(8,128)(2,1)S(1)}, bf16[1536,256]{1,0:T(8,128)(2,1)S(1)}, u32[]{:S(2)}, u32[]{:S(2)}) collective-permute-start(bf16[1536,256]{1,0:T(8,128)(2,1)S(1)} %get-tuple-element.16), channel_id=1, source_target_pairs={{0,1},{1,0},{2,3},{3,2},{4,5},{5,4},{6,7},{7,6},{8,9},{9,8},{10,11... | collective-permute-start | bytes 2359304 | tf_op jit(solution)/shard_map/ppermute | solution.py:31
  67.6 2.2 %collective-permute-start.1 = (bf16[1024,256]{1,0:T(8,128)(2,1)S(1)}, bf16[1024,256]{1,0:T(8,128)(2,1)S(1)}, u32[]{:S(2)}, u32[]{:S(2)}) collective-permute-start(bf16[1024,256]{1,0:T(8,128)(2,1)S(1)} %get-tuple-element.17), channel_id=1, source_target_pairs={{0,1},{1,0},{2,3},{3,2},{4,5},{5,4},{6,7},{7,6},{8,9},{9,8},{10,11... | collective-permute-start | bytes 1572872 | tf_op jit(solution)/shard_map/ppermute | solution.py:31

commit v7 on v6

--- a/solution.py
+++ b/solution.py
@@ -93,7 +93,7 @@
     return afters, steer.reshape(mats * 2, rows, width // 2)
 
 
-def gram_kernel(group, x, own, sent):
+def gram_kernel(group, x, own):
     start = 0
     for j in group:
         value = lax.dot_general(
@@ -105,7 +105,6 @@
         at = slice(start, start + (j + 1) * TILE)
         start += (j + 1) * TILE
         own[at] = value
-        sent[at] = value.astype(jnp.bfloat16)
 
 
 def gram_half(x, group, pairs):
@@ -113,10 +112,7 @@
     shape = (len(pairs) * TILE, TILE)
     return pl.pallas_call(
         functools.partial(gram_kernel, group),
-        out_shape=(
-            jax.ShapeDtypeStruct(shape, jnp.float32),
-            jax.ShapeDtypeStruct(shape, jnp.bfloat16),
-        ),
+        out_shape=jax.ShapeDtypeStruct(shape, jnp.float32),
         in_specs=[pl.BlockSpec(memory_space=pltpu.VMEM)],
         compiler_params=pltpu.CompilerParams(vmem_limit_bytes=16 * MIB),
         cost_estimate=cost(2 * len(pairs) * TILE * TILE * part, rows * part * 2 + len(pairs) * TILE * TILE * 6),
@@ -127,7 +123,7 @@
 def update_kernel(x, *rest):
     owns, others, rest = rest[: len(GROUPS)], rest[len(GROUPS) : 2 * len(GROUPS)], rest[2 * len(GROUPS) :]
     afters = rest[:AFTER_PARTS]
-    out, stored, g, h, s, w, m0, m1, after_sem = rest[AFTER_PARTS:]
+    out, stored, g, h, s, w, m0, m1, wide0, wide1, after_sem = rest[AFTER_PARTS:]
     storing = []
     for c, after in enumerate(afters):
         share = after.shape[0]
@@ -140,7 +136,8 @@
     total = jnp.zeros((1, 1), jnp.float32)
     for own, other, pairs in zip(owns, others, PAIRS):
         for k, (i, j) in enumerate(pairs):
-            block = own[span(k)] + other[span(k)].astype(jnp.float32)
+            block = own[span(k)] + other[span(k)]
+            wide0[span(i), span(j)] = block
             narrow = block.astype(jnp.bfloat16)
             g[span(i), span(j)] = narrow
             if i == j:
@@ -154,12 +151,14 @@
     direct = LINEAR**3 * factor
     square = inverse * inverse
 
-    def product(left, right, store, rest):
+    def product(left, right, store, rest, keep=None):
         lost = [None] * SIDE
         for j in reversed(range(SIDE)):
             at = (slice(0, (j + 1) * TILE), span(j))
             value = jnp.dot(left[at[0], :], right[:, at[1]], preferred_element_type=jnp.float32)
             value = rest(value, at, j)
+            if keep is not None:
+                keep[at] = value
             narrow = value.astype(jnp.bfloat16)
             store[at] = narrow
             for i in range(j):
@@ -172,11 +171,11 @@
 
 
     product(g, g, m0, lambda v, at, j: square * (CUBIC * wide(g, at) + square * (QUINTIC * v)))
-    product(m0, g, w, lambda v, at, j: square * (LINEAR * wide(g, at) + v))
-    product(m0, w, h, lambda v, at, j: LINEAR * wide(w, at) + v)
+    product(m0, g, w, lambda v, at, j: square * (LINEAR * wide0[at] + v), wide1)
+    product(m0, w, h, lambda v, at, j: LINEAR * wide1[at] + v, wide0)
     product(h, h, m1, lambda v, at, j: CUBIC * wide(h, at) + QUINTIC * v)
-    product(m1, h, w, lambda v, at, j: LINEAR * wide(h, at) + v)
-    product(m1, w, g, lambda v, at, j: LINEAR * wide(w, at) + v)
+    product(m1, h, w, lambda v, at, j: LINEAR * wide0[at] + v, wide1)
+    product(m1, w, g, lambda v, at, j: LINEAR * wide1[at] + v)
     lost = product(m1, m0, s, lambda v, at, j: LINEAR * (wide(m0, at) + wide(m1, at)) + v)
     across = [jnp.sum(block, axis=0, keepdims=True) for block in lost]
     down = [LINEAR * jnp.sum(block, axis=1, keepdims=True) for block in lost]
@@ -211,6 +210,7 @@
         out_specs=(inside, anywhere),
         scratch_shapes=[
             *[square] * 6,
+            *[pltpu.VMEM((n, n), jnp.float32)] * 2,
             pltpu.SemaphoreType.DMA((AFTER_PARTS,)),
         ],
         compiler_params=pltpu.CompilerParams(vmem_limit_bytes=30 * MIB),
@@ -231,9 +231,9 @@
     x = exchange(pieces).reshape(count * rows, half)
     owns, others = [], []
     for group, pairs in zip(GROUPS, PAIRS):
-        own, sent = gram_half(x, group, pairs)
+        own = gram_half(x, group, pairs)
         owns.append(own)
-        others.append(partner(sent, "fsdp", 0))
+        others.append(partner(own, "fsdp", 0))
     outgoing, new_momentum = update_half(x, owns, others, afters)
     returned = exchange(outgoing.reshape(count, rows, half))
     update = returned.reshape(mats, 2, rows, half).transpose(0, 2, 1, 3).reshape(mats, rows, width)

time: 139 us -> 141 us (1.014)
  no operation moved by 1% of the time
where the time goes in v7:
time: 141 us
  blocking collectives  109 us (77%)
  Pallas kernels  24.5 us (17%)
  waiting for transfers between devices  3.11 us (2%)
  local copies, waits for them, and re-layouts  1.84 us (1%)
  starting transfers between devices  1.67 us (1%)
    all_to_all x2, blocking collectives, exchange(): return lax.all_to_all(x, 'fsdp', split_axis=0, concat_axis=0, tiled=True)  109 us
    pallas_call x1, Pallas kernels, update_half(): pl.pallas_call(update_kernel, out_shape=(jax.ShapeDtypeStruct((n, part),...  17.3 us
    pallas_call x1, Pallas kernels, steer_pieces(): pl.pallas_call(steer_kernel, out_shape=(*[quarter] * AFTER_PARTS, jax.Sha...  4.46 us
    ppermute x2, waiting for transfers between devices, partner(): lax.ppermute(x, axis, [(i, i ^ 1 << apart) for i in range(lax.axis_size(a...  3.11 us
  transfers between devices with their start and end apart: 2, of which 1 were waited for; matrix products, arithmetic and copies ran while one was open for 0% of the time, Pallas kernels for 1%

profile of v7, /device:TPU:1, one launch (start us, length us, event | category | flops | bytes accessed | tf_op | source)
XLA Modules:
  0.0 140.6 jit_solution(8557227293825299009)
XLA Ops:
  0.6 4.5 %steer.1 = (f32[16,8,3584]{2,1,0:T(8,128)S(1)}, f32[16,8,3584]{2,1,0:T(8,128)S(1)}, f32[16,8,3584]{2,1,0:T(8,128)S(1)}, f32[16,8,3584]{2,1,0:T(8,128)S(1)}, bf16[64,2,8,1792]{3,2,1,0:T(8,128)(2,1)S(1)}) custom-call(f32[64,8,3584]{2,1,0:T(8,128)} %momentum.1, bf16[64,8,3584]{2,1,0:T(8,128)(2,1)} %gradient.1), custom_call_target="tpu_custom_call" | custom-call | flops 7340032 | bytes 14680064 | tf_op jit(solution)/shard_map/steer/pallas_call | solution.py:80
  5.1 58.4 %all_to_all.10 = bf16[128,8,1792]{2,1,0:T(8,128)(2,1)S(1)} all-to-all(bf16[128,8,1792]{2,1,0:T(8,128)(2,1)S(1)} %bitcast.12), channel_id=1, replica_groups=mesh['fsdp'=128] {'fsdp'}, dimensions={0} | all-to-all | bytes 7340032 | tf_op jit(solution)/shard_map/all_to_all | solution.py:223
  63.5 1.6 %gram.2.rest_0_ = f32[1536,256]{1,0:T(8,128)S(1)} custom-call(bf16[1024,1792]{1,0:T(8,128)(2,1)S(1)} %bitcast.8), custom_call_target="tpu_custom_call" | custom-call | flops 1409286144 | bytes 6029312 | tf_op jit(solution)/shard_map/gram/pallas_call | solution.py:113
  65.1 1.4 collective-permute-start
  66.5 1.1 gram.3.rest_1_
  67.6 0.3 collective-permute-start.1
  67.9 3.1 %collective-permute-done.1.rest_3_ = f32[1024,256]{1,0:T(8,128)S(1)} collective-permute-done((f32[1024,256]{1,0:T(8,128)S(1)}, f32[1024,256]{1,0:T(8,128)S(1)}, u32[]{:S(2)}, u32[]{:S(2)}) %collective-permute-start.1) | collective-permute-done | bytes 1048608 | tf_op jit(solution)/shard_map/ppermute | solution.py:31
  71.0 0.0 collective-permute-done.rest_2_
  71.0 17.3 %update.1 = (bf16[1024,1792]{1,0:T(8,128)(2,1)S(1)}, f32[64,8,3584]{2,1,0:T(8,128)}) custom-call(bf16[1024,1792]{1,0:T(8,128)(2,1)S(1)} %bitcast.10, f32[1536,256]{1,0:T(8,128)S(1)} %gram.2.rest_0_, f32[1024,256]{1,0:T(8,128)S(1)} %gram.3.rest_1_, f32[1536,256]{1,0:T(8,128)S(1)} %collective-permute-done.rest_2_, ...), custom_call_target="tpu_custom_call" | custom-call | flops 23085449216 | bytes 13631488 | tf_op jit(solution)/shard_map/update/pallas_call | solution.py:203
  88.3 50.5 %all_to_all.11 = bf16[128,8,1792]{2,1,0:T(8,128)(2,1)S(1)} all-to-all(bf16[128,8,1792]{2,1,0:T(8,128)(2,1)S(1)} %bitcast.11), channel_id=1, replica_groups=mesh['fsdp'=128] {'fsdp'}, dimensions={0} | all-to-all | bytes 7340032 | tf_op jit(solution)/shard_map/all_to_all | solution.py:223
  138.8 1.8 %copy.5 = bf16[64,8,3584]{2,1,0:T(8,128)(2,1)} copy(bf16[64,8,3584]{2,1,0:T(8,128)(2,1)S(1)} %bitcast.13) | data formatting | bytes 7340032
Async XLA Ops:
  65.1 5.9 %collective-permute-start = (f32[1536,256]{1,0:T(8,128)S(1)}, f32[1536,256]{1,0:T(8,128)S(1)}, u32[]{:S(2)}, u32[]{:S(2)}) collective-permute-start(f32[1536,256]{1,0:T(8,128)S(1)} %gram.2.rest_0_), channel_id=1, source_target_pairs={{0,1},{1,0},{2,3},{3,2},{4,5},{5,4},{6,7},{7,6},{8,9},{9,8},{10,11... | collective-permute-start | bytes 4718600 | tf_op jit(solution)/shard_map/ppermute | solution.py:31
  67.6 3.4 %collective-permute-start.1 = (f32[1024,256]{1,0:T(8,128)S(1)}, f32[1024,256]{1,0:T(8,128)S(1)}, u32[]{:S(2)}, u32[]{:S(2)}) collective-permute-start(f32[1024,256]{1,0:T(8,128)S(1)} %gram.3.rest_1_), channel_id=1, source_target_pairs={{0,1},{1,0},{2,3},{3,2},{4,5},{5,4},{6,7},{7,6},{8,9},{9,8},{10,11... | collective-permute-start | bytes 3145736 | tf_op jit(solution)/shard_map/ppermute | solution.py:31

commit v8 on v7

--- a/solution.py
+++ b/solution.py
@@ -14,6 +14,7 @@
 FACTOR = 0.2 * max(FF, D) ** 0.5
 TILE = 256
 SIDE = FF // TILE
+HALF = TILE // 2
 GROUPS = [(2, 1, 0), (3,)]
 PAIRS = [[(i, j) for j in group for i in range(j + 1)] for group in GROUPS]
 MIB = 2**20
@@ -93,8 +94,16 @@
     return afters, steer.reshape(mats * 2, rows, width // 2)
 
 
+def starts(group):
+    found = [0]
+    for j in group:
+        for i in range(j + 1):
+            found.append(found[-1] + (HALF if i == j else TILE) + TILE)
+    return found
+
+
 def gram_kernel(group, x, own):
-    start = 0
+    places = dict(zip(((i, j) for j in group for i in range(j + 1)), starts(group)))
     for j in group:
         value = lax.dot_general(
             x[0 : (j + 1) * TILE],
@@ -102,14 +111,16 @@
             (((1,), (1,)), ((), ())),
             preferred_element_type=jnp.float32,
         )
-        at = slice(start, start + (j + 1) * TILE)
-        start += (j + 1) * TILE
-        own[at] = value
+        for i in range(j + 1):
+            block, first = value[span(i)], places[i, j]
+            left = HALF if i == j else TILE
+            own[first : first + left] = block[:left, :HALF]
+            own[first + left : first + left + TILE] = block[:, HALF:]
 
 
 def gram_half(x, group, pairs):
     rows, part = x.shape
-    shape = (len(pairs) * TILE, TILE)
+    shape = (starts(group)[-1], HALF)
     return pl.pallas_call(
         functools.partial(gram_kernel, group),
         out_shape=jax.ShapeDtypeStruct(shape, jnp.float32),
@@ -134,18 +145,26 @@
         jnp.int32, (TILE, TILE), 1
     )
     total = jnp.zeros((1, 1), jnp.float32)
-    for own, other, pairs in zip(owns, others, PAIRS):
-        for k, (i, j) in enumerate(pairs):
-            block = own[span(k)] + other[span(k)]
-            wide0[span(i), span(j)] = block
-            narrow = block.astype(jnp.bfloat16)
-            g[span(i), span(j)] = narrow
+    for own, other, pairs, group in zip(owns, others, PAIRS, GROUPS):
+        for (i, j), first in zip(pairs, starts(group)):
+            left = HALF if i == j else TILE
+            row, column = i * TILE, j * TILE
+            near = own[first : first + left] + other[first : first + left]
+            at = slice(first + left, first + left + TILE)
+            far = own[at] + other[at]
+            corners = ((row, column, near), (row, column + HALF, far))
             if i == j:
-                block = jnp.where(here, block, 0.0)
-                block = jnp.sum(block, axis=0, keepdims=True)
-                total = total + jnp.sum(block, axis=1, keepdims=True)
-            else:
-                g[span(j), span(i)] = narrow.T
+                for block in (near, far[HALF:]):
+                    block = jnp.where(here[:HALF, :HALF], block, 0.0)
+                    block = jnp.sum(block, axis=0, keepdims=True)
+                    total = total + jnp.sum(block, axis=1, keepdims=True)
+                corners = (*corners, (row + HALF, column, far[:HALF].T))
+            for r, c, block in corners:
+                at = (slice(r, r + block.shape[0]), slice(c, c + HALF))
+                wide0[at] = block
+                g[at] = block.astype(jnp.bfloat16)
+                if i != j:
+                    g[at[1], at[0]] = block.astype(jnp.bfloat16).T
     inverse = 1.0 / (jnp.sqrt(total) + 1e-07)
     factor = inverse * FACTOR
     direct = LINEAR**3 * factor

time: 141 us -> 141 us (level)
  no operation moved by 1% of the time
where the time goes in v8:
time: 141 us
  blocking collectives  109 us (77%)
  Pallas kernels  24.8 us (18%)
  waiting for transfers between devices  2.74 us (2%)
  local copies, waits for them, and re-layouts  1.84 us (1%)
  starting transfers between devices  1.67 us (1%)
    all_to_all x2, blocking collectives, exchange(): return lax.all_to_all(x, 'fsdp', split_axis=0, concat_axis=0, tiled=True)  109 us
    pallas_call x1, Pallas kernels, update_half(): pl.pallas_call(update_kernel, out_shape=(jax.ShapeDtypeStruct((n, part),...  17.6 us
    pallas_call x1, Pallas kernels, steer_pieces(): pl.pallas_call(steer_kernel, out_shape=(*[quarter] * AFTER_PARTS, jax.Sha...  4.46 us
  transfers between devices with their start and end apart: 2, of which 1 were waited for; matrix products, arithmetic and copies ran while one was open for 0% of the time, Pallas kernels for 1%

profile of v8, /device:TPU:1, one launch (start us, length us, event | category | flops | bytes accessed | tf_op | source)
XLA Modules:
  0.0 140.6 jit_solution(2180400522325016880)
XLA Ops:
  0.6 4.5 %steer.1 = (f32[16,8,3584]{2,1,0:T(8,128)S(1)}, f32[16,8,3584]{2,1,0:T(8,128)S(1)}, f32[16,8,3584]{2,1,0:T(8,128)S(1)}, f32[16,8,3584]{2,1,0:T(8,128)S(1)}, bf16[64,2,8,1792]{3,2,1,0:T(8,128)(2,1)S(1)}) custom-call(f32[64,8,3584]{2,1,0:T(8,128)} %momentum.1, bf16[64,8,3584]{2,1,0:T(8,128)(2,1)} %gradient.1), custom_call_target="tpu_custom_call" | custom-call | flops 7340032 | bytes 14680064 | tf_op jit(solution)/shard_map/steer/pallas_call | solution.py:81
  5.1 58.4 %all_to_all.10 = bf16[128,8,1792]{2,1,0:T(8,128)(2,1)S(1)} all-to-all(bf16[128,8,1792]{2,1,0:T(8,128)(2,1)S(1)} %bitcast.12), channel_id=1, replica_groups=mesh['fsdp'=128] {'fsdp'}, dimensions={0} | all-to-all | bytes 7340032 | tf_op jit(solution)/shard_map/all_to_all | solution.py:242
  63.5 1.6 %gram.2.rest_0_ = f32[2688,128]{1,0:T(8,128)S(1)} custom-call(bf16[1024,1792]{1,0:T(8,128)(2,1)S(1)} %bitcast.8), custom_call_target="tpu_custom_call" | custom-call | flops 1409286144 | bytes 6029312 | tf_op jit(solution)/shard_map/gram/pallas_call | solution.py:124
  65.1 1.4 collective-permute-start
  66.5 1.1 gram.3.rest_1_
  67.6 0.3 collective-permute-start.1
  67.9 2.7 %collective-permute-done.1.rest_3_ = f32[1920,128]{1,0:T(8,128)S(1)} collective-permute-done((f32[1920,128]{1,0:T(8,128)S(1)}, f32[1920,128]{1,0:T(8,128)S(1)}, u32[]{:S(2)}, u32[]{:S(2)}) %collective-permute-start.1) | collective-permute-done | bytes 983072 | tf_op jit(solution)/shard_map/ppermute | solution.py:32
  70.6 0.0 collective-permute-done.rest_2_
  70.6 17.6 %update.1 = (bf16[1024,1792]{1,0:T(8,128)(2,1)S(1)}, f32[64,8,3584]{2,1,0:T(8,128)}) custom-call(bf16[1024,1792]{1,0:T(8,128)(2,1)S(1)} %bitcast.10, f32[2688,128]{1,0:T(8,128)S(1)} %gram.2.rest_0_, f32[1920,128]{1,0:T(8,128)S(1)} %gram.3.rest_1_, f32[2688,128]{1,0:T(8,128)S(1)} %collective-permute-done.rest_2_, ...), custom_call_target="tpu_custom_call" | custom-call | flops 23085449216 | bytes 13631488 | tf_op jit(solution)/shard_map/update/pallas_call | solution.py:222
  88.2 50.5 %all_to_all.11 = bf16[128,8,1792]{2,1,0:T(8,128)(2,1)S(1)} all-to-all(bf16[128,8,1792]{2,1,0:T(8,128)(2,1)S(1)} %bitcast.11), channel_id=1, replica_groups=mesh['fsdp'=128] {'fsdp'}, dimensions={0} | all-to-all | bytes 7340032 | tf_op jit(solution)/shard_map/all_to_all | solution.py:242
  138.7 1.8 %copy.5 = bf16[64,8,3584]{2,1,0:T(8,128)(2,1)} copy(bf16[64,8,3584]{2,1,0:T(8,128)(2,1)S(1)} %bitcast.13) | data formatting | bytes 7340032
Async XLA Ops:
  65.1 5.6 %collective-permute-start = (f32[2688,128]{1,0:T(8,128)S(1)}, f32[2688,128]{1,0:T(8,128)S(1)}, u32[]{:S(2)}, u32[]{:S(2)}) collective-permute-start(f32[2688,128]{1,0:T(8,128)S(1)} %gram.2.rest_0_), channel_id=1, source_target_pairs={{0,1},{1,0},{2,3},{3,2},{4,5},{5,4},{6,7},{7,6},{8,9},{9,8},{10,11... | collective-permute-start | bytes 4128776 | tf_op jit(solution)/shard_map/ppermute | solution.py:32
  67.6 3.0 %collective-permute-start.1 = (f32[1920,128]{1,0:T(8,128)S(1)}, f32[1920,128]{1,0:T(8,128)S(1)}, u32[]{:S(2)}, u32[]{:S(2)}) collective-permute-start(f32[1920,128]{1,0:T(8,128)S(1)} %gram.3.rest_1_), channel_id=1, source_target_pairs={{0,1},{1,0},{2,3},{3,2},{4,5},{5,4},{6,7},{7,6},{8,9},{9,8},{10,11... | collective-permute-start | bytes 2949128 | tf_op jit(solution)/shard_map/ppermute | solution.py:32
